TPU v7x, 32 devices: a whole 2x2x4 slice. The times are simulated.
32 devices in a mesh: gx: 8 (over z, y), gy: 4 (over x, core).
Axes of the slice: x: 2, y: 2, z: 4, core: 2. Of those that a mesh axis runs over, the one named last changes fastest.
Arguments:
- rate_x: float32 [40, 64, 512], P(None, 'gx', 'gy'), may hold values from 0.0025 to 0.25
- rate_y: float32 [40, 64, 512], P(None, 'gx', 'gy'), may hold values from 0.00015625 to 0.015625
- land_mask: int32 [64, 512], P('gx', 'gy'), may hold values 0 or 1
- obs_cell: int32 [32, 32, 32], P(('gx', 'gy')), may hold values from 0 to 81919
- obs_count: int32 [32, 32], P(('gx', 'gy')), may hold values from 0 to 32, as said below
- innovation: float32 [32, 32, 32], P(('gx', 'gy')), may hold values from -12 to 12
- obs_weight: float32 [32, 4, 256, 256], P(('gx', 'gy')), may hold values from -9 to 9, as said below
Outputs:
- solution: float32 [2, 40, 64, 512], P(None, None, 'gx', 'gy')
- residual: float32 [2, 40, 64, 512], P(None, None, 'gx', 'gy')
Inputs may be any that keep to these rules, and one draw needn't show every extreme that they name: obs_count[s, d] slots of pair (s, d) hold observations, slots 0 to obs_count[s, d] - 1; in every draw some owner d has obs_count[s, d] = 32 for every source s. Each block obs_weight[s, n] is symmetric positive definite.
All inputs are finite; a program needn't handle non-finite values. No bound on the sum of `land_mask` on one device may be relied on, other than what follows from the above.
Results may differ from a plain program's by a relative error of at most 0.0003.
Values sent between devices are 32-bit elements; how exact they have to be, the bound alone decides.
A program may use at most 128 MiB of HBM per device.

v0:
```python
import jax
import jax.numpy as jnp
from jax import lax
from jax.sharding import PartitionSpec as P

TR = 2
ITERS = 2


def entering_2(part, axis, combine, identity, reverse):
    count = lax.axis_size(axis)
    place = lax.axis_index(axis)
    ahead = count - 1 - place if reverse else place
    gathered = jax.tree.map(lambda a: lax.all_gather(a, axis), part)
    state = jax.tree.map(lambda a, e: jnp.zeros_like(a) + jnp.asarray(e, a.dtype), part, identity)

    def one(lap, state):
        source = count - 1 - lap if reverse else lap
        return combine(
            state, jax.tree.map(lambda a: lax.dynamic_index_in_dim(a, source, 0, False), gathered)
        )

    return lax.fori_loop(0, ahead, one, state)


def from_root(value, axis, source):
    kept = jnp.where(lax.axis_index(axis) == source, value, 0).astype(value.dtype)
    return lax.psum(kept, axis)


def compose_maps(earlier, following):
    return (earlier[0] * following[0], following[0] * earlier[1] + following[1])


def shift_along(values, distance, line_axis, reverse, filler):
    length = values.shape[line_axis]
    edge_shape = list(values.shape)
    edge_shape[line_axis] = distance
    edge = jnp.full(tuple(edge_shape), filler, values.dtype)
    if reverse:
        return jnp.concatenate(
            [lax.slice_in_dim(values, distance, length, axis=line_axis), edge], axis=line_axis
        )
    return jnp.concatenate(
        [edge, lax.slice_in_dim(values, 0, length - distance, axis=line_axis)], axis=line_axis
    )


def factor_levels(retention, line_axis, reverse):
    length = retention.shape[line_axis]
    stored = []
    factor = retention
    distance = 1
    while distance < length:
        stored.append(factor)
        factor = factor * shift_along(factor, distance, line_axis, reverse, 1.0)
        distance = distance * 2
    return (stored, factor)


def scan_offsets(stored, forcing, line_axis, reverse):
    distance = 1
    for level_factor in stored:
        forcing = forcing + level_factor * shift_along(forcing, distance, line_axis, reverse, 0.0)
        distance = distance * 2
    return forcing


def local_maps(direction_plan, forcing, line_axis, reverse):
    stored, overall = direction_plan
    return (overall, scan_offsets(stored, forcing, line_axis, reverse))


def make_plan(decay_rate, line_axis):
    retention = jnp.exp(-decay_rate)[None]
    one_minus = -jnp.expm1(-decay_rate)
    scaling = jnp.sqrt(one_minus * (1.0 + jnp.exp(-decay_rate)))
    weight = jnp.sqrt(jnp.sqrt(one_minus))
    return (
        retention,
        scaling,
        weight,
        factor_levels(retention, line_axis, False),
        factor_levels(retention, line_axis, True),
    )


def carry_x(totals, reverse):
    identity_map = (jnp.ones_like(totals[0]), jnp.zeros_like(totals[1]))
    before = entering_2(totals, "gx", compose_maps, identity_map, reverse)
    through = compose_maps(before, totals)
    root_index = 0 if reverse else lax.axis_size("gx") - 1
    stacked = from_root(jnp.stack(through), "gx", root_index)
    closure = (stacked[0], stacked[1])
    start_state = closure[1] / (1.0 - closure[0])
    return before[1] + before[0] * start_state


def carry_y(totals, reverse):
    identity_map = (jnp.ones_like(totals[0]), jnp.zeros_like(totals[1]))
    before = entering_2(totals, "gy", compose_maps, identity_map, reverse)
    return before[1]


def shifted_next(back_factor, back_offset, line_axis):
    line_length = back_factor.shape[line_axis]
    next_factor = jnp.concatenate(
        [
            lax.slice_in_dim(back_factor, 1, line_length, axis=line_axis),
            jnp.ones_like(lax.slice_in_dim(back_factor, 0, 1, axis=line_axis)),
        ],
        axis=line_axis,
    )
    next_offset = jnp.concatenate(
        [
            lax.slice_in_dim(back_offset, 1, line_length, axis=line_axis),
            jnp.zeros_like(lax.slice_in_dim(back_offset, 0, 1, axis=line_axis)),
        ],
        axis=line_axis,
    )
    return (next_factor, next_offset)


def line_operator(state_field, line_plan, line_axis, carry_fn):
    retention, scaling, weight, forward_plan, backward_plan = line_plan
    line_length = state_field.shape[line_axis]
    factor, offset = local_maps(forward_plan, scaling * weight * state_field, line_axis, False)
    last_offset = lax.index_in_dim(offset, line_length - 1, line_axis, keepdims=False)
    totals = (
        jnp.broadcast_to(
            lax.index_in_dim(factor, line_length - 1, line_axis, keepdims=False), last_offset.shape
        ),
        last_offset,
    )
    entering = jnp.expand_dims(carry_fn(totals, False), line_axis)
    forward = offset + factor * entering
    back_factor, back_offset = local_maps(backward_plan, retention * forward, line_axis, True)
    first_offset = lax.index_in_dim(back_offset, 0, line_axis, keepdims=False)
    totals = (
        jnp.broadcast_to(
            lax.index_in_dim(back_factor, 0, line_axis, keepdims=False), first_offset.shape
        ),
        first_offset,
    )
    entering = jnp.expand_dims(carry_fn(totals, True), line_axis)
    next_factor, next_offset = shifted_next(back_factor, back_offset, line_axis)
    return weight * scaling * (forward + next_offset + next_factor * entering)


def global_dot(first_field, second_field):
    return lax.psum(jnp.sum(first_field * second_field), ("gx", "gy"))


def on_device(rate_x, rate_y, land_mask, obs_cell, obs_count, innovation, obs_weight):
    ocean = land_mask.astype(jnp.float32)
    field_shape = (TR,) + rate_x.shape
    plan_along_x = make_plan(rate_x, 2)
    plan_along_y = make_plan(rate_y, 3)

    def along_x(state_field):
        return line_operator(state_field, plan_along_x, 2, carry_x)

    def along_y(state_field):
        return line_operator(state_field, plan_along_y, 3, carry_y)

    def gather_back(vector):
        return ocean * along_x(along_y(ocean * vector))

    cell_index = obs_cell[0]
    occupied = (
        lax.broadcasted_iota(jnp.int32, cell_index.shape, 1) < obs_count[0][:, None]
    ).astype(jnp.float32)
    blocks = obs_weight[0]

    def weigh_obs(values):
        packed = (occupied * values).reshape(blocks.shape[0], blocks.shape[1])
        mixed = jnp.einsum("nij,nj->ni", blocks, packed, precision=lax.Precision.HIGHEST)
        return occupied * mixed.reshape(occupied.shape)

    def deposit(values):
        arrived = lax.all_to_all(values, ("gx", "gy"), split_axis=0, concat_axis=0, tiled=True)
        flat_cells = (
            jnp.zeros((TR * rate_x.size,), jnp.float32)
            .at[cell_index.reshape(-1)]
            .add(arrived.reshape(-1))
        )
        return flat_cells.reshape(field_shape)

    right_side = gather_back(deposit(weigh_obs(innovation[0])))
    solution = jnp.zeros_like(right_side)
    residual = right_side
    direction = right_side
    norm_now = global_dot(residual, residual)
    for iteration in range(ITERS):
        picked = jnp.take(
            (ocean * along_y(along_x(ocean * direction))).reshape(-1),
            cell_index.reshape(-1),
            axis=0,
        ).reshape(cell_index.shape)
        hessian_dir = direction + gather_back(
            deposit(
                weigh_obs(
                    lax.all_to_all(picked, ("gx", "gy"), split_axis=0, concat_axis=0, tiled=True)
                )
            )
        )
        step_length = norm_now / global_dot(direction, hessian_dir)
        solution = solution + step_length * direction
        residual = residual - step_length * hessian_dir
        norm_next = global_dot(residual, residual)
        direction = residual + norm_next / norm_now * direction
        norm_now = norm_next
    return (solution, residual)


def solution(mesh):
    placed = (
        P(None, "gx", "gy"),
        P(None, "gx", "gy"),
        P("gx", "gy"),
        P(("gx", "gy"), None, None),
        P(("gx", "gy"), None),
        P(("gx", "gy"), None, None),
        P(("gx", "gy"), None, None, None),
    )
    return jax.shard_map(
        on_device,
        mesh=mesh,
        in_specs=placed,
        out_specs=(P(None, None, "gx", "gy"), P(None, None, "gx", "gy")),
        check_vma=False,
    )
```

profile of v0, /device:TPU:0, one launch (start us, length us, event | category | flops | bytes accessed | tf_op | source)
XLA Modules:
  0.0 1598.9 jit_solution(17275373734198495516)
XLA Ops:
  13.1 7.4 all-to-all-start
  29.0 33.0 %all-gather.4 = f32[8,40,1,128]{3,1,2,0:T(8,128)} all-gather(f32[1,40,1,128]{3,1,2,0:T(8,128)S(1)} %bitcast.584), channel_id=10, replica_groups=mesh['gx'=8,'gy'=4] {'gx'}, dimensions={0}, use_global_device_ids=true | all-gather | bytes 184320 | tf_op jit(solution)/shard_map/all_gather | solution.py:14
  76.3 5.2 all-gather
  81.5 5.6 all-gather.2
  87.6 2.0 reduce.19
  90.4 6.8 scatter_custom_fusion
  103.5 5.2 all-gather.1
  112.4 12.0 all-gather.3
  124.4 1.8 copy.452
  129.3 33.3 %all-gather.5 = f32[16,40,1,128]{3,1,2,0:T(8,128)} all-gather(f32[2,40,1,128]{3,1,2,0:T(8,128)S(1)} %bitcast.613), channel_id=11, replica_groups=mesh['gx'=8,'gy'=4] {'gx'}, dimensions={0}, use_global_device_ids=true | all-gather | bytes 368640 | tf_op jit(solution)/shard_map/all_gather | solution.py:14
  167.2 37.6 %all-gather.6 = f32[8,40,1,128]{3,1,2,0:T(8,128)} all-gather(f32[1,40,1,128]{3,1,2,0:T(8,128)S(1)} %bitcast.590), channel_id=12, replica_groups=mesh['gx'=8,'gy'=4] {'gx'}, dimensions={0}, use_global_device_ids=true | all-gather | bytes 184320 | tf_op jit(solution)/shard_map/all_gather | solution.py:14
  204.8 34.0 %all-reduce.144.cloned.1.call-done = f32[2,2,40,128]{3,2,1,0:T(8,128)} async-done(((f32[2,2,40,128]{3,2,1,0:T(8,128)}), f32[2,2,40,128]{3,2,1,0:T(8,128)}) %all-reduce.144.cloned.1.call-update) | async-done | bytes 81936 | tf_op jit(solution)/shard_map/psum | solution.py:28
  241.7 32.9 %all-gather.7 = f32[16,40,1,128]{3,1,2,0:T(8,128)} all-gather(f32[2,40,1,128]{3,1,2,0:T(8,128)S(1)} %slice_bitcast_fusion.6), channel_id=13, replica_groups=mesh['gx'=8,'gy'=4] {'gx'}, dimensions={0}, use_global_device_ids=true | all-gather | bytes 368640 | tf_op jit(solution)/shard_map/all_gather | solution.py:14
  274.7 5.8 while.263
  284.9 63.3 %all-reduce.146.cloned.1.call-done = f32[2,2,40,128]{3,2,1,0:T(8,128)} async-done(((f32[2,2,40,128]{3,2,1,0:T(8,128)}), f32[2,2,40,128]{3,2,1,0:T(8,128)}) %all-reduce.146.cloned.1.call-update) | async-done | bytes 81936 | tf_op jit(solution)/shard_map/psum | solution.py:28
  351.9 32.9 %all-gather.8 = f32[16,40,1,128]{3,1,2,0:T(8,128)} all-gather(f32[2,40,1,128]{3,1,2,0:T(8,128)S(1)} %slice_bitcast_fusion.5), channel_id=14, replica_groups=mesh['gx'=8,'gy'=4] {'gx'}, dimensions={0}, use_global_device_ids=true | all-gather | bytes 368640 | tf_op jit(solution)/shard_map/all_gather | solution.py:14
  387.7 77.9 %all-reduce.148.cloned.1.call-done = f32[2,2,40,128]{3,2,1,0:T(8,128)} async-done(((f32[2,2,40,128]{3,2,1,0:T(8,128)}), f32[2,2,40,128]{3,2,1,0:T(8,128)}) %all-reduce.148.cloned.1.call-update) | async-done | bytes 81936 | tf_op jit(solution)/shard_map/psum | solution.py:28
  467.6 32.9 %all-gather.9 = f32[16,40,1,128]{3,1,2,0:T(8,128)} all-gather(f32[2,40,1,128]{3,1,2,0:T(8,128)S(1)} %slice_bitcast_fusion.4), channel_id=15, replica_groups=mesh['gx'=8,'gy'=4] {'gx'}, dimensions={0}, use_global_device_ids=true | all-gather | bytes 368640 | tf_op jit(solution)/shard_map/all_gather | solution.py:14
  501.1 10.0 while.265
  516.3 62.5 %all-reduce.150.cloned.1.call-done = f32[2,2,40,128]{3,2,1,0:T(8,128)} async-done(((f32[2,2,40,128]{3,2,1,0:T(8,128)}), f32[2,2,40,128]{3,2,1,0:T(8,128)}) %all-reduce.150.cloned.1.call-update) | async-done | bytes 81936 | tf_op jit(solution)/shard_map/psum | solution.py:28
  583.4 11.9 all-gather.10
  595.3 1.8 copy.483
  600.8 12.9 all-gather.11
  613.7 1.8 copy.485
  615.5 2.1 while.267
  619.2 6.2 gather_fusion
  626.0 10.4 all_to_all.42
  639.0 2.5 all-to-all-start.2
  641.6 7.0 all-to-all-done.2
  649.4 6.8 scatter_custom_fusion.1
  660.7 11.5 all-gather.12
  672.2 1.8 copy.491
  677.9 13.4 all-gather.13
  691.3 1.8 copy.493
  693.1 2.1 while.269
  697.6 32.9 %all-gather.14 = f32[16,40,1,128]{3,1,2,0:T(8,128)} all-gather(f32[2,40,1,128]{3,1,2,0:T(8,128)S(1)} %slice_bitcast_fusion.3), channel_id=20, replica_groups=mesh['gx'=8,'gy'=4] {'gx'}, dimensions={0}, use_global_device_ids=true | all-gather | bytes 368640 | tf_op jit(solution)/shard_map/all_gather | solution.py:14
  732.6 75.3 %all-reduce.152.cloned.1.call-done = f32[2,2,40,128]{3,2,1,0:T(8,128)} async-done(((f32[2,2,40,128]{3,2,1,0:T(8,128)}), f32[2,2,40,128]{3,2,1,0:T(8,128)}) %all-reduce.152.cloned.1.call-update) | async-done | bytes 81936 | tf_op jit(solution)/shard_map/psum | solution.py:28
  809.8 32.9 %all-gather.15 = f32[16,40,1,128]{3,1,2,0:T(8,128)} all-gather(f32[2,40,1,128]{3,1,2,0:T(8,128)S(1)} %slice_bitcast_fusion.2), channel_id=21, replica_groups=mesh['gx'=8,'gy'=4] {'gx'}, dimensions={0}, use_global_device_ids=true | all-gather | bytes 368640 | tf_op jit(solution)/shard_map/all_gather | solution.py:14
  843.4 10.0 while.271
  856.6 64.4 %all-reduce.154.cloned.1.call-done = f32[2,2,40,128]{3,2,1,0:T(8,128)} async-done(((f32[2,2,40,128]{3,2,1,0:T(8,128)}), f32[2,2,40,128]{3,2,1,0:T(8,128)}) %all-reduce.154.cloned.1.call-update) | async-done | bytes 81936 | tf_op jit(solution)/shard_map/psum | solution.py:28
  921.9 2.5 multiply_reduce_fusion.2
  924.4 40.3 %all-reduce.132 = (f32[]{:T(128)}, f32[]{:T(128)}) all-reduce(f32[]{:T(128)} %get-tuple-element.1522, f32[]{:T(128)} %get-tuple-element.1520), channel_id=1, replica_groups=mesh['gx'=8,'gy'=4] {'gx','gy'}, use_global_device_ids=true, to_apply=%region_12.13 | all-reduce | flops 2 | bytes 16 | tf_op jit(solution)/shard_map/psum | solution.py:151
  967.7 39.5 %psum.106 = f32[]{:T(128)} all-reduce(f32[]{:T(128)} %multiply_reduce_fusion.1), channel_id=1, replica_groups=mesh['gx'=8,'gy'=4] {'gx','gy'}, use_global_device_ids=true, to_apply=%region_37.39 | all-reduce | flops 1 | bytes 8 | tf_op jit(solution)/shard_map/psum | solution.py:151
  1010.0 32.9 %all-gather.16 = f32[16,40,1,128]{3,1,2,0:T(8,128)} all-gather(f32[2,40,1,128]{3,1,2,0:T(8,128)S(1)} %slice_bitcast_fusion.1), channel_id=22, replica_groups=mesh['gx'=8,'gy'=4] {'gx'}, dimensions={0}, use_global_device_ids=true | all-gather | bytes 368640 | tf_op jit(solution)/shard_map/all_gather | solution.py:14
  1043.7 75.5 %all-reduce.156.cloned.1.call-done = f32[2,2,40,128]{3,2,1,0:T(8,128)} async-done(((f32[2,2,40,128]{3,2,1,0:T(8,128)}), f32[2,2,40,128]{3,2,1,0:T(8,128)}) %all-reduce.156.cloned.1.call-update) | async-done | bytes 81936 | tf_op jit(solution)/shard_map/psum | solution.py:28
  1121.9 32.9 %all-gather.17 = f32[16,40,1,128]{3,1,2,0:T(8,128)} all-gather(f32[2,40,1,128]{3,1,2,0:T(8,128)S(1)} %slice_bitcast_fusion), channel_id=23, replica_groups=mesh['gx'=8,'gy'=4] {'gx'}, dimensions={0}, use_global_device_ids=true | all-gather | bytes 368640 | tf_op jit(solution)/shard_map/all_gather | solution.py:14
  1154.9 6.0 while.273
  1164.0 64.4 %all-reduce.158.cloned.1.call-done = f32[2,2,40,128]{3,2,1,0:T(8,128)} async-done(((f32[2,2,40,128]{3,2,1,0:T(8,128)}), f32[2,2,40,128]{3,2,1,0:T(8,128)}) %all-reduce.158.cloned.1.call-update) | async-done | bytes 81936 | tf_op jit(solution)/shard_map/psum | solution.py:28
  1238.3 5.2 all-gather.18
  1248.0 13.9 all-gather.19
  1261.9 1.8 copy.528
  1265.6 6.2 gather_fusion.1
  1272.5 11.4 all_to_all.43
  1287.1 2.5 all-to-all-start.4
  1289.7 7.0 all-to-all-done.4
  1297.5 6.1 scatter_custom_fusion.2
  1310.6 5.2 all-gather.20
  1320.0 13.0 all-gather.21
  1337.5 30.9 %all-gather.22 = f32[16,40,1,128]{3,1,2,0:T(8,128)S(1)} all-gather(f32[2,40,1,128]{3,1,2,0:T(8,128)S(1)} %bitcast.611), channel_id=28, replica_groups=mesh['gx'=8,'gy'=4] {'gx'}, dimensions={0}, use_global_device_ids=true | all-gather | bytes 368640 | tf_op jit(solution)/shard_map/all_gather | solution.py:14
  1369.2 72.1 %all-reduce.160.cloned.1.call-done = f32[2,2,40,128]{3,2,1,0:T(8,128)} async-done(((f32[2,2,40,128]{3,2,1,0:T(8,128)}), f32[2,2,40,128]{3,2,1,0:T(8,128)}) %all-reduce.160.cloned.1.call-update) | async-done | bytes 81936 | tf_op jit(solution)/shard_map/psum | solution.py:28
  1443.7 31.1 %all-gather.23 = f32[16,40,1,128]{3,1,2,0:T(8,128)S(1)} all-gather(f32[2,40,1,128]{3,1,2,0:T(8,128)S(1)} %bitcast.609), channel_id=29, replica_groups=mesh['gx'=8,'gy'=4] {'gx'}, dimensions={0}, use_global_device_ids=true | all-gather | bytes 368640 | tf_op jit(solution)/shard_map/all_gather | solution.py:14
  1474.7 5.8 while.279
  1481.3 66.1 %all-reduce.162.cloned.1.call-done = f32[2,2,40,128]{3,2,1,0:T(8,128)} async-done(((f32[2,2,40,128]{3,2,1,0:T(8,128)}), f32[2,2,40,128]{3,2,1,0:T(8,128)}) %all-reduce.162.cloned.1.call-update) | async-done | bytes 81936 | tf_op jit(solution)/shard_map/psum | solution.py:28
  1548.9 40.3 %psum.111 = f32[]{:T(128)} all-reduce(f32[]{:T(128)} %multiply_reduce_fusion), channel_id=1, replica_groups=mesh['gx'=8,'gy'=4] {'gx','gy'}, use_global_device_ids=true, to_apply=%region_60.62 | all-reduce | flops 1 | bytes 8 | tf_op jit(solution)/shard_map/psum | solution.py:151
  (801 shorter events, 193.6 us)
Async XLA Ops:
  7.2 3.5 copy-start
  7.2 13.4 copy-start.109
  13.1 74.0 %all-to-all-start = ((f32[32,1,32]{2,1,0:T(1,128)}), f32[32,1,32]{2,1,0:T(1,128)}, u32[]{:S(2)}, u32[]{:S(2)}) async-start(f32[32,1,32]{2,1,0:T(1,128)} %fusion.85), calls=%async_computation | async-start | bytes 32768 | tf_op jit(solution)/shard_map/all_to_all | solution.py:181
  20.6 218.3 %all-reduce.144.cloned.1.call-start = ((), (), s32[]{:S(2)}) async-start(), calls=%async_computation.5 | async-start | bytes 163840 | tf_op jit(solution)/shard_map/psum | solution.py:28
  22.6 39.4 %copy-start.98 = (f32[1,40,8,128]{3,2,1,0:T(8,128)}, f32[1,40,8,128]{3,2,1,0:T(8,128)S(1)}, u32[]{:S(2)}) copy-start(f32[1,40,8,128]{3,2,1,0:T(8,128)S(1)} %pad_multiply_fusion.41) | copy-start | bytes 491524
  23.7 1.7 copy-start.110
  26.3 37.6 %copy-start.85 = (f32[1,40,8,128]{3,2,1,0:T(8,128)}, f32[1,40,8,128]{3,2,1,0:T(8,128)S(1)}, u32[]{:S(2)}) copy-start(f32[1,40,8,128]{3,2,1,0:T(8,128)S(1)} %get-tuple-element.1551) | copy-start | bytes 491524
  26.3 37.6 %copy-start.123 = (s32[8,128]{1,0:T(8,128)S(1)}, s32[8,128]{1,0:T(8,128)}, u32[]{:S(2)}) copy-start(s32[8,128]{1,0:T(8,128)} %param.51) | copy-start | bytes 12292
  29.0 133.7 %copy-start.101 = (f32[1,40,1,128]{3,2,1,0:T(1,128)}, f32[1,40,1,128]{3,2,1,0:T(1,128)S(1)}, u32[]{:S(2)}) copy-start(f32[1,40,1,128]{3,2,1,0:T(1,128)S(1)} %slice.772) | copy-start | bytes 61444
  67.0 34.5 %copy-start.37 = (f32[40,8,128]{2,0,1:T(8,128)}, f32[40,8,128]{2,0,1:T(8,128)S(1)}, u32[]{:S(2)}) copy-start(f32[40,8,128]{2,0,1:T(8,128)S(1)} %copy.428) | copy-start | bytes 491524
  67.0 34.8 %copy-start.32 = (f32[40,8,128]{2,0,1:T(8,128)}, f32[40,8,128]{2,0,1:T(8,128)S(1)}, u32[]{:S(2)}) copy-start(f32[40,8,128]{2,0,1:T(8,128)S(1)} %copy.431) | copy-start | bytes 491524
  67.1 35.1 %copy-start.27 = (f32[40,8,128]{2,0,1:T(8,128)}, f32[40,8,128]{2,0,1:T(8,128)S(1)}, u32[]{:S(2)}) copy-start(f32[40,8,128]{2,0,1:T(8,128)S(1)} %copy.434) | copy-start | bytes 491524
  67.3 43.8 %copy-start.16 = (f32[40,8,128]{2,0,1:T(8,128)}, f32[40,8,128]{2,0,1:T(8,128)S(1)}, u32[]{:S(2)}) copy-start(f32[40,8,128]{2,0,1:T(8,128)S(1)} %copy.443) | copy-start | bytes 491524
  67.3 43.9 %copy-start.11 = (f32[40,8,128]{2,0,1:T(8,128)}, f32[40,8,128]{2,0,1:T(8,128)S(1)}, u32[]{:S(2)}) copy-start(f32[40,8,128]{2,0,1:T(8,128)S(1)} %copy.444) | copy-start | bytes 491524
  67.4 44.1 %copy-start.6 = (f32[40,8,128]{2,0,1:T(8,128)}, f32[40,8,128]{2,0,1:T(8,128)S(1)}, u32[]{:S(2)}) copy-start(f32[40,8,128]{2,0,1:T(8,128)S(1)} %copy.445) | copy-start | bytes 491524
  67.4 609.1 %copy-start.3 = (f32[40,8,128]{2,0,1:T(8,128)}, f32[40,8,128]{2,0,1:T(8,128)S(1)}, u32[]{:S(2)}) copy-start(f32[40,8,128]{2,0,1:T(8,128)S(1)} %copy.446) | copy-start | bytes 491524
  67.5 609.3 %copy-start.1 = (f32[40,8,128]{2,0,1:T(8,128)}, f32[40,8,128]{2,0,1:T(8,128)S(1)}, u32[]{:S(2)}) copy-start(f32[40,8,128]{2,0,1:T(8,128)S(1)} %copy.447) | copy-start | bytes 491524
  70.5 56.0 %copy-start.23 = (f32[40,8,128]{2,0,1:T(8,128)}, f32[40,8,128]{2,0,1:T(8,128)S(1)}, u32[]{:S(2)}) copy-start(f32[40,8,128]{2,0,1:T(8,128)S(1)} %copy.450) | copy-start | bytes 491524
  97.2 1.3 copy-start.80
  112.4 13.8 copy-start.116
  128.3 34.3 %copy-start.111 = (f32[8,40,1,128]{3,1,2,0:T(8,128)S(1)}, f32[8,40,1,128]{3,1,2,0:T(8,128)}, u32[]{:S(2)}) copy-start(f32[8,40,1,128]{3,1,2,0:T(8,128)} %all-gather.4) | copy-start | bytes 491524
  129.2 33.4 %copy-start.93 = (f32[2,40,8,128]{3,2,1,0:T(8,128)}, f32[2,40,8,128]{3,2,1,0:T(8,128)S(1)}, u32[]{:S(2)}) copy-start(f32[2,40,8,128]{3,2,1,0:T(8,128)S(1)} %copy_add_fusion.23) | copy-start | bytes 983044
  162.7 2.5 copy-start.75
  162.7 3.4 copy-start.86
  163.4 184.8 %all-reduce.146.cloned.1.call-start = ((), (), s32[]{:S(2)}) async-start(), calls=%async_computation.6 | async-start | bytes 163840 | tf_op jit(solution)/shard_map/psum | solution.py:28
  164.4 116.1 %copy-start.104 = (f32[1,40,1,128]{3,2,1,0:T(1,128)}, f32[1,40,1,128]{3,2,1,0:T(1,128)S(1)}, u32[]{:S(2)}) copy-start(f32[1,40,1,128]{3,2,1,0:T(1,128)S(1)} %slice.784) | copy-start | bytes 61444
  166.2 74.9 %copy-start.69 = (f32[40,8,128]{2,0,1:T(8,128)}, f32[40,8,128]{2,0,1:T(8,128)S(1)}, u32[]{:S(2)}) copy-start(f32[40,8,128]{2,0,1:T(8,128)S(1)} %copy.472) | copy-start | bytes 491524
  167.2 74.4 %copy-start.64 = (f32[40,8,128]{2,0,1:T(8,128)}, f32[40,8,128]{2,0,1:T(8,128)S(1)}, u32[]{:S(2)}) copy-start(f32[40,8,128]{2,0,1:T(8,128)S(1)} %copy.473) | copy-start | bytes 491524
  241.5 33.1 %copy-start.112 = (f32[8,40,1,128]{3,1,2,0:T(8,128)S(1)}, f32[8,40,1,128]{3,1,2,0:T(8,128)}, u32[]{:S(2)}) copy-start(f32[8,40,1,128]{3,1,2,0:T(8,128)} %all-gather.6) | copy-start | bytes 491524
  241.7 32.9 %copy-start.94 = (f32[2,40,8,128]{3,1,0,2:T(8,128)}, f32[2,40,8,128]{3,1,0,2:T(8,128)S(1)}, u32[]{:S(2)}) copy-start(f32[2,40,8,128]{3,1,0,2:T(8,128)S(1)} %multiply_add_fusion.71) | copy-start | bytes 983044
  280.5 1.5 copy-start.74
  282.1 183.6 %all-reduce.148.cloned.1.call-start = ((), (), s32[]{:S(2)}) async-start(), calls=%async_computation.7 | async-start | bytes 163840 | tf_op jit(solution)/shard_map/psum | solution.py:28
  386.9 191.9 %all-reduce.150.cloned.1.call-start = ((), (), s32[]{:S(2)}) async-start(), calls=%async_computation.8 | async-start | bytes 163840 | tf_op jit(solution)/shard_map/psum | solution.py:28
  467.6 32.9 %copy-start.95 = (f32[2,40,8,128]{3,1,0,2:T(8,128)}, f32[2,40,8,128]{3,1,0,2:T(8,128)S(1)}, u32[]{:S(2)}) copy-start(f32[2,40,8,128]{3,1,0,2:T(8,128)S(1)} %multiply_add_fusion.64) | copy-start | bytes 983044
  579.7 1.4 copy-start.53
  617.7 1.5 copy-start.118
  619.2 18.0 %copy-start.120 = (pred[4,256]{1,0:T(4,128)(4,1)S(1)}, pred[4,256]{1,0:T(4,128)(4,1)}, u32[]{:S(2)}) copy-start(pred[4,256]{1,0:T(4,128)(4,1)} %get-tuple-element.1527) | copy-start | bytes 3076
  619.2 19.1 %copy-start.122 = (s32[1,32]{1,0:T(1,128)S(1)}, s32[1,32]{1,0:T(1,128)}, u32[]{:S(2)}) copy-start(s32[1,32]{1,0:T(1,128)} %param.53) | copy-start | bytes 388
  625.3 30.8 %copy-start.21 = (f32[40,8,128]{2,0,1:T(8,128)S(1)}, f32[40,8,128]{2,0,1:T(8,128)}, u32[]{:S(2)}) copy-start(f32[40,8,128]{2,0,1:T(8,128)} %copy.414) | copy-start | bytes 491524
  638.1 20.2 %copy-start.54 = (f32[40,8,128]{2,0,1:T(8,128)S(1)}, f32[40,8,128]{2,0,1:T(8,128)}, u32[]{:S(2)}) copy-start(f32[40,8,128]{2,0,1:T(8,128)} %copy.419) | copy-start | bytes 491524
  639.0 9.6 all-to-all-start.2
  641.5 166.4 %all-reduce.152.cloned.1.call-start = ((), (), s32[]{:S(2)}) async-start(), calls=%async_computation.9 | async-start | bytes 163840 | tf_op jit(solution)/shard_map/psum | solution.py:28
  657.2 1.4 copy-start.49
  677.9 17.3 %copy-start.22 = (f32[40,8,128]{2,0,1:T(8,128)S(1)}, f32[40,8,128]{2,0,1:T(8,128)}, u32[]{:S(2)}) copy-start(f32[40,8,128]{2,0,1:T(8,128)} %copy.414) | copy-start | bytes 491524
  677.9 17.3 %copy-start.24 = (f32[40,8,128]{2,0,1:T(8,128)S(1)}, f32[40,8,128]{2,0,1:T(8,128)}, u32[]{:S(2)}) copy-start(f32[40,8,128]{2,0,1:T(8,128)} %copy-done.23) | copy-start | bytes 491524
  732.5 188.5 %all-reduce.154.cloned.1.call-start = ((), (), s32[]{:S(2)}) async-start(), calls=%async_computation.10 | async-start | bytes 163840 | tf_op jit(solution)/shard_map/psum | solution.py:28
  809.8 32.9 %copy-start.96 = (f32[2,40,8,128]{3,1,0,2:T(8,128)}, f32[2,40,8,128]{3,1,0,2:T(8,128)S(1)}, u32[]{:S(2)}) copy-start(f32[2,40,8,128]{3,1,0,2:T(8,128)S(1)} %multiply_add_fusion.27) | copy-start | bytes 983044
  854.9 264.3 %all-reduce.156.cloned.1.call-start = ((), (), s32[]{:S(2)}) async-start(), calls=%async_computation.11 | async-start | bytes 163840 | tf_op jit(solution)/shard_map/psum | solution.py:28
  1010.0 33.0 %copy-start.102 = (f32[1,40,1,128]{3,2,1,0:T(1,128)S(1)}, f32[1,40,1,128]{3,2,1,0:T(1,128)}, u32[]{:S(2)}) copy-start(f32[1,40,1,128]{3,2,1,0:T(1,128)} %copy-done.101) | copy-start | bytes 61444
  1043.6 184.8 %all-reduce.158.cloned.1.call-start = ((), (), s32[]{:S(2)}) async-start(), calls=%async_computation.12 | async-start | bytes 163840 | tf_op jit(solution)/shard_map/psum | solution.py:28
  1121.1 33.7 %copy-start.97 = (f32[2,40,8,128]{3,1,0,2:T(8,128)}, f32[2,40,8,128]{3,1,0,2:T(8,128)S(1)}, u32[]{:S(2)}) copy-start(f32[2,40,8,128]{3,1,0,2:T(8,128)S(1)} %multiply_add_fusion.18) | copy-start | bytes 983044
  1121.1 39.7 %copy-start.105 = (f32[1,40,1,128]{3,2,1,0:T(1,128)S(1)}, f32[1,40,1,128]{3,2,1,0:T(1,128)}, u32[]{:S(2)}) copy-start(f32[1,40,1,128]{3,2,1,0:T(1,128)} %copy-done.104) | copy-start | bytes 61444
  1229.3 1.4 copy-start.81
  1248.0 15.7 copy-start.91
  1248.0 16.2 %copy-start.25 = (f32[40,8,128]{2,0,1:T(8,128)S(1)}, f32[40,8,128]{2,0,1:T(8,128)}, u32[]{:S(2)}) copy-start(f32[40,8,128]{2,0,1:T(8,128)} %copy-done.23) | copy-start | bytes 491524
  1264.2 1.4 copy-start.119
  1265.6 19.1 %copy-start.121 = (pred[4,256]{1,0:T(4,128)(4,1)S(1)}, pred[4,256]{1,0:T(4,128)(4,1)}, u32[]{:S(2)}) copy-start(pred[4,256]{1,0:T(4,128)(4,1)} %get-tuple-element.1527) | copy-start | bytes 3076
  1287.1 9.6 all-to-all-start.4
  1289.7 151.6 %all-reduce.160.cloned.1.call-start = ((), (), s32[]{:S(2)}) async-start(), calls=%async_computation.13 | async-start | bytes 163840 | tf_op jit(solution)/shard_map/psum | solution.py:28
  1320.0 15.0 copy-start.26
  1337.3 31.1 %copy-start.103 = (f32[1,40,1,128]{3,2,1,0:T(1,128)S(1)}, f32[1,40,1,128]{3,2,1,0:T(1,128)}, u32[]{:S(2)}) copy-start(f32[1,40,1,128]{3,2,1,0:T(1,128)} %copy-done.101) | copy-start | bytes 61444
  1369.2 178.3 %all-reduce.162.cloned.1.call-start = ((), (), s32[]{:S(2)}) async-start(), calls=%async_computation.14 | async-start | bytes 163840 | tf_op jit(solution)/shard_map/psum | solution.py:28
  1443.4 37.2 %copy-start.106 = (f32[1,40,1,128]{3,2,1,0:T(1,128)S(1)}, f32[1,40,1,128]{3,2,1,0:T(1,128)}, u32[]{:S(2)}) copy-start(f32[1,40,1,128]{3,2,1,0:T(1,128)} %copy-done.104) | copy-start | bytes 61444
  1480.6 110.0 %copy-start.76 = (f32[2,40,8,128]{3,1,0,2:T(8,128)S(1)}, f32[2,40,8,128]{3,1,0,2:T(8,128)}, u32[]{:S(2)}) copy-start(f32[2,40,8,128]{3,1,0,2:T(8,128)} %get-tuple-element.1521) | copy-start | bytes 983044
  (73 other events, 64.0 us)
Sparse Core Ops, SparseCore 0:
  163.5 75.2 all-reduce.143
  282.2 65.9 all-reduce.145
  387.0 78.5 all-reduce.147
  512.8 66.0 all-reduce.149
  732.7 75.1 all-reduce.151
  855.0 66.0 all-reduce.153
  1043.7 75.4 all-reduce.155
  1162.4 65.9 all-reduce.157
  1369.3 71.9 all-reduce.159
  1481.4 65.9 all-reduce.161
where the time goes:
time: 1610 us; the launch traced here: 1600 us
  waiting for transfers between devices  670 us (42%)
  blocking collectives  653 us (41%)
  other arithmetic  135 us (8%)
  local copies, waits for them, and re-layouts  102 us (6%)
  between operations  22.1 us (1%)
    psum x10, waiting for transfers between devices, from_root(): return lax.psum(kept, axis)  656 us
    all_gather x24, blocking collectives, entering_2(): gathered = jax.tree.map(lambda a: lax.all_gather(a, axis), part)  511 us
    psum x3, blocking collectives, global_dot(): return lax.psum(jnp.sum(first_field * second_field), ('gx', 'gy'))  120 us
    add x50, other arithmetic, compose_maps(): return (earlier[0] * following[0], following[0] * earlier[1] + following[1])  41.4 us
    unnamed x285, local copies, waits for them, and re-layouts  33.8 us
  transfers between devices with their start and end apart: 13, of which 12 were waited for; matrix products, arithmetic and copies ran while one was open for 2% of the time, Pallas kernels for 0%

commit v1 on v0

v1 whole, which is shorter than its diff:
```python
import functools

import jax
import jax.numpy as jnp
from jax import lax
from jax.experimental import pallas as pl
from jax.experimental.pallas import tpu as pltpu
from jax.sharding import PartitionSpec as P

TR = 2
ITERS = 2
SUB = 8
LANE = 128
GL = 8
MESH = pl.DeviceIdType.MESH
F32 = jnp.float32
BF16 = jnp.bfloat16


def split3(a):
    hi = a.astype(BF16)
    rest = a - hi.astype(F32)
    mid = rest.astype(BF16)
    lo = (rest - mid.astype(F32)).astype(BF16)
    return hi, mid, lo


def kernel(
    nx, ny, lev, slots,
    dx, wx, dy, wy, ocean_ref, cell, occ, innov, wobs,
    sol, res,
    drn, v, ob, qb, fld, ffx, fbx, k1x, k2x, ffy, fby, k1y, k2y,
    ex, xx, rows1h, lanes1h, yold, xinv, xown,
    as_, ar, xs1, xr1, xs2, xr2, ys, yr,
    a_ss, a_rs, x1_ss, x1_rs, x2_ss, x2_rs, y_ss, y_rs,
):
    nodes = nx * ny
    per = LANE // slots
    nch = nodes * slots // LANE
    rr_rows = TR * lev // nx
    R = rr_rows
    G = lev // GL
    mx = lax.axis_index("gx")
    my = lax.axis_index("gy")
    me = mx * ny + my
    NXP = 2 * ITERS + 1

    barrier = pltpu.get_barrier_semaphore()

    def greet(off, c):
        d = lax.rem(me + off, nodes)
        pl.semaphore_signal(barrier, inc=1, device_id=(d // ny, lax.rem(d, ny)), device_id_type=MESH)
        return c

    lax.fori_loop(1, nodes, greet, 0)

    sub_i = lax.broadcasted_iota(jnp.int32, (GL, SUB, LANE), 1)
    lane_i = lax.broadcasted_iota(jnp.int32, (GL, SUB, LANE), 2)
    four = (TR, GL, SUB, LANE)
    tag = (
        lax.broadcasted_iota(jnp.int32, four, 3)
        - lax.broadcasted_iota(jnp.int32, four, 0) * lev
        - lax.broadcasted_iota(jnp.int32, four, 1)
    )
    ocean = ocean_ref[...]

    def steps(n):
        out, s = [], 1
        while s < n:
            out.append(s)
            s *= 2
        return out

    def scan(a, fac, lv, n, axis, back, g):
        for k, s in enumerate(steps(n)):
            a = a + fac[k, pl.ds(GL * g, GL)] * pltpu.roll(a, (n - s) if back else s, axis)
        return a

    def coefficients(d_ref, w_ref, ff, fb, k1, k2, n, ax, g):
        at = pl.ds(GL * g, GL)
        i = sub_i if ax == 1 else lane_i
        d = d_ref[at]
        w = w_ref[at]
        p = d
        b = d
        for k, s in enumerate(steps(n)):
            ff[k, at] = jnp.where(i >= s, p, 0.0)
            p = p * jnp.where(i >= s, pltpu.roll(p, s, ax), 1.0)
            fb[k, at] = jnp.where(i < n - s, b, 0.0)
            b = b * jnp.where(i < n - s, pltpu.roll(b, n - s, ax), 1.0)
        c = scan(d * p, fb, None, n, ax, True, g)
        k1[at] = w * (p + jnp.where(i < n - 1, pltpu.roll(c, n - 1, ax), 0.0))
        k2[at] = w * jnp.where(i < n - 1, pltpu.roll(b, n - 1, ax), 1.0)
        return p, c

    def put_rows(ref, a, g):
        for t in range(TR):
            start = pl.multiple_of((t * lev + GL * g) * SUB, GL * SUB)
            ref[pl.ds(start, GL * SUB), :] = a[t].reshape(GL * SUB, LANE)

    def local_x(u, g):
        at = pl.ds(GL * g, GL)
        w = wx[at]
        o = scan(w * u, ffx, None, SUB, 2, False, g)
        q = scan(dx[at] * o, fbx, None, SUB, 2, True, g)
        v[:, at] = w * (o + jnp.where(sub_i < SUB - 1, pltpu.roll(q, SUB - 1, 2), 0.0))
        put_rows(ob, o, g)
        put_rows(qb, q, g)

    def pick(a, col, g):
        column = jnp.broadcast_to(a[..., col : col + 1], four)
        return jnp.sum(jnp.where(tag == GL * g, column, 0.0), axis=(0, 1))

    def local_y(u, g):
        at = pl.ds(GL * g, GL)
        w = wy[at]
        o = scan(w * u, ffy, None, LANE, 3, False, g)
        q = scan(dy[at] * o, fby, None, LANE, 3, True, g)
        v[:, at] = w * (o + jnp.where(lane_i < LANE - 1, pltpu.roll(q, LANE - 1, 3), 0.0))
        return pick(o, LANE - 1, g), pick(q, 0, g)

    def after_x(g):
        at = pl.ds(GL * g, GL)

        def rows(ref):
            parts = [ref[pl.ds(pl.multiple_of(t * lev + GL * g, GL), GL), :] for t in range(TR)]
            return jnp.stack([p.reshape(GL, 1, LANE) for p in parts])

        return v[:, at] + k1x[at] * rows(ex) + k2x[at] * rows(xx)

    def after_y(e, x, g):
        at = pl.ds(GL * g, GL)

        def column(a):
            return jnp.sum(jnp.where(tag == GL * g, a, 0.0), axis=3, keepdims=True)

        return v[:, at] + k1y[at] * column(e) + k2y[at] * column(x)

    zero = jnp.zeros((SUB, LANE), F32)

    def wait_all(buf, sem):
        pltpu.make_async_copy(buf, buf, sem).wait()

    def x_start(src, dst, ss, rs, p):
        def one(off, c):
            j = lax.rem(mx + off, nx)
            pltpu.make_async_remote_copy(
                src_ref=src.at[p, j], dst_ref=dst.at[p, mx], send_sem=ss.at[p], recv_sem=rs.at[p],
                device_id=(j, my), device_id_type=MESH,
            ).start()
            return c

        lax.fori_loop(1, nx, one, 0)
        dst[p, mx] = src[p, mx]

    def x_wait(src, dst, ss, rs, p):
        wait_all(dst.at[p, pl.ds(0, nx - 1)], rs.at[p])
        wait_all(src.at[p, pl.ds(0, nx - 1)], ss.at[p])

    def x_fill(p, row):
        for j in range(nx):
            xs1[p, j, 0:R] = ob[pl.ds(SUB - 1 + SUB * R * j, R, stride=SUB), :]
            xs1[p, j, R : 2 * R] = qb[pl.ds(SUB * R * j, R, stride=SUB), :]
            xs1[p, j, 2 * R : 2 * R + 1] = row

    def x_exchange(p, row):
        x_fill(p, row)
        x_start(xs1, xr1, x1_ss, x1_rs, p)
        x_wait(xs1, xr1, x1_ss, x1_rs, p)
        A = [xown[j, 0:R] for j in range(nx)]
        C = [xown[j, R : 2 * R] for j in range(nx)]
        F = [xr1[p, j, 0:R] for j in range(nx)]
        B = [xr1[p, j, R : 2 * R] for j in range(nx)]
        inv = xinv[0:R]
        e = F[0]
        for j in range(1, nx):
            e = F[j] + A[j] * e
        e = e * inv
        gs = []
        for j in range(nx):
            xs2[p, j, 0:R] = e
            gs.append(B[j] + C[j] * e)
            e = F[j] + A[j] * e
        x = gs[nx - 1]
        for j in range(nx - 2, -1, -1):
            x = gs[j] + A[j] * x
        x = x * inv
        for j in range(nx - 1, -1, -1):
            xs2[p, j, R : 2 * R] = x
            x = gs[j] + A[j] * x
        x_start(xs2, xr2, x2_ss, x2_rs, p)
        total = xr1[p, 0, 2 * R : 2 * R + 1]
        for j in range(1, nx):
            total = total + xr1[p, j, 2 * R : 2 * R + 1]
        x_wait(xs2, xr2, x2_ss, x2_rs, p)
        for j in range(nx):
            ex[R * j : R * (j + 1)] = xr2[p, j, 0:R]
            xx[R * j : R * (j + 1)] = xr2[p, j, R : 2 * R]
        return total

    def y_start(p, f, b, row):
        ys[p, 0:SUB] = f
        ys[p, SUB : 2 * SUB] = b
        ys[p, 2 * SUB : 3 * SUB] = jnp.broadcast_to(row, (SUB, LANE))

        def one(off, c):
            j = lax.rem(my + off, ny)
            pltpu.make_async_remote_copy(
                src_ref=ys.at[p], dst_ref=yr.at[p, my], send_sem=y_ss.at[p], recv_sem=y_rs.at[p],
                device_id=(mx, j), device_id_type=MESH,
            ).start()
            return c

        lax.fori_loop(1, ny, one, 0)
        yr[p, my] = ys[p]

    def y_wait(p):
        wait_all(yr.at[p, pl.ds(0, ny - 1)], y_rs.at[p])
        wait_all(yr.at[p, pl.ds(0, ny - 1)], y_ss.at[p])

    def y_exchange(p, f, b, row):
        y_start(p, f, b, row)
        y_wait(p)
        total = yr[p, 0, 2 * SUB : 2 * SUB + 1]
        for j in range(1, ny):
            total = total + yr[p, j, 2 * SUB : 2 * SUB + 1]
        e, mine_e, gs = zero, zero, []
        for j in range(ny):
            mine_e = jnp.where(my == j, e, mine_e)
            gs.append(yr[p, j, SUB : 2 * SUB] + yr[NXP, j, SUB : 2 * SUB] * e)
            e = yr[p, j, 0:SUB] + yr[NXP, j, 0:SUB] * e
        x, mine_x = zero, zero
        for j in range(ny - 1, -1, -1):
            mine_x = jnp.where(my == j, x, mine_x)
            x = gs[j] + yr[NXP, j, 0:SUB] * x
        return mine_e, mine_x, total

    def a_start(p, chunks):
        for c in range(nch):
            as_[p, c] = chunks[c]

        def one(off, c):
            d = lax.rem(me + off, nodes)
            pltpu.make_async_remote_copy(
                src_ref=as_.at[p, d // per], dst_ref=ar.at[p, me], send_sem=a_ss.at[p], recv_sem=a_rs.at[p],
                device_id=(d // ny, lax.rem(d, ny)), device_id_type=MESH,
            ).start()
            return c

        lax.fori_loop(1, nodes, one, 0)
        ar[p, me] = as_[p, me // per]

    def a_wait(p):
        wait_all(ar.at[p, pl.ds(0, nodes - 1)], a_rs.at[p])
        wait_all(ar.at[p, pl.ds(0, nodes - 1)], a_ss.at[p])
        got = ar[p].reshape(nch, per, 1, LANE)
        block = lax.broadcasted_iota(jnp.int32, (nch, 1, LANE), 2) // slots
        mine = lax.rem(me, per)
        total = jnp.zeros((nch, 1, LANE), F32)
        for i in range(per):
            turned = pltpu.roll(got[:, i], lax.rem(i - mine + per, per) * slots, 2)
            total = jnp.where(block == i, turned, total)
        return total

    def weigh(y):
        y = occ[...] * y
        per_block = wobs.shape[1] // LANE
        chunks = []
        for n in range(wobs.shape[0]):
            row = jnp.concatenate([y[per_block * n + a] for a in range(per_block)], axis=1)
            z = lax.dot_general(
                jnp.broadcast_to(row, (SUB, row.shape[1])), wobs[n], (((1,), (1,)), ((), ())),
                precision=lax.Precision.HIGHEST, preferred_element_type=F32,
            )
            for a in range(per_block):
                chunks.append(z[0:1, a * LANE : (a + 1) * LANE] * occ[per_block * n + a])
        return chunks

    def onehots():
        ri = lax.broadcasted_iota(jnp.int32, (TR * lev * SUB, LANE), 0)
        li = lax.broadcasted_iota(jnp.int32, (LANE, LANE), 0)
        for c in range(nch):
            here = cell[c]
            cols = slice(c * LANE, (c + 1) * LANE)
            rows1h[:, cols] = jnp.where(ri == here // LANE, 1.0, 0.0).astype(BF16)
            lanes1h[:, cols] = jnp.where(li == lax.rem(here, LANE), 1.0, 0.0)

    def observe():
        t = jnp.transpose(fld[...].reshape(TR * lev * SUB, LANE))
        lhs = jnp.concatenate(split3(t), axis=0)
        chunks = []
        for c in range(nch):
            cols = slice(c * LANE, (c + 1) * LANE)
            got = jnp.dot(lhs, rows1h[:, cols], preferred_element_type=F32)
            got = (got[0:LANE] + got[LANE : 2 * LANE]) + got[2 * LANE :]
            chunks.append(jnp.sum(got * lanes1h[:, cols], axis=0, keepdims=True))
        return chunks

    def deposit(vals):
        row = jnp.concatenate([vals[c] for c in range(nch)], axis=1)
        rhs = jnp.concatenate(split3(lanes1h[...] * row), axis=0)
        got = lax.dot_general(rows1h[...], rhs, (((1,), (1,)), ((), ())), preferred_element_type=F32)
        got = (got[:, 0:LANE] + got[:, LANE : 2 * LANE]) + got[:, 2 * LANE :]
        fld[...] = got.reshape(TR, lev, SUB, LANE)

    def lane_total(row):
        return jnp.broadcast_to(jnp.sum(row, axis=1, keepdims=True), (1, LANE))

    def fold(tile):
        return jnp.sum(tile, axis=0, keepdims=True)

    def forth(p, row, body):
        vals = a_wait(p)
        deposit(vals)

        def first(g, c):
            f, b = local_y(ocean * fld[:, pl.ds(GL * g, GL)], g)
            return c[0] + f, c[1] + b

        f, b = lax.fori_loop(0, G, first, (zero, zero))
        e, x, total = y_exchange(p, f, b, row)

        def second(g, c):
            local_x(after_y(e, x, g), g)
            return c

        lax.fori_loop(0, G, second, 0)
        total = lane_total(x_exchange(p, total))
        return fold(lax.fori_loop(0, G, lambda g, c: body(g, c, ocean * after_x(g), total), zero))

    def back(p, row, body):
        def first(g, c):
            local_x(ocean * res[:, pl.ds(GL * g, GL)], g)
            return c

        lax.fori_loop(0, G, first, 0)
        total = x_exchange(p, row)

        def second(g, c):
            f, b = local_y(after_x(g), g)
            return c[0] + f, c[1] + b

        f, b = lax.fori_loop(0, G, second, (zero, zero))
        e, x, total = y_exchange(p, f, b, total)
        total = lane_total(total)

        def third(g, c):
            fld[:, pl.ds(GL * g, GL)] = ocean * after_y(e, x, g)
            return body(g, c, total)

        dd = fold(lax.fori_loop(0, G, third, zero))
        a_start(p, observe())
        return a_wait(p), dd, total

    for buf in (xs1, xs2):
        buf[...] = jnp.zeros(buf.shape, F32)
    chunks = weigh(innov[...])
    pl.semaphore_wait(barrier, nodes - 1)
    a_start(0, chunks)

    def prepare(g, c):
        p, b = coefficients(dx, wx, ffx, fbx, k1x, k2x, SUB, 1, g)
        put_rows(ob, [p] * TR, g)
        put_rows(qb, [b] * TR, g)
        p, b = coefficients(dy, wy, ffy, fby, k1y, k2y, LANE, 2, g)
        p = jnp.broadcast_to(p[None], four)
        b = jnp.broadcast_to(b[None], four)
        return c[0] + pick(p, LANE - 1, g), c[1] + pick(b, 0, g)

    a, c = lax.fori_loop(0, G, prepare, (zero, zero))
    y_start(NXP, a, c, zero[0:1])
    x_fill(NXP, zero[0:1])
    x_start(xs1, xr1, x1_ss, x1_rs, NXP)
    onehots()
    y_wait(NXP)
    x_wait(xs1, xr1, x1_ss, x1_rs, NXP)
    xown[...] = xr1[NXP]
    whole = xown[0, 0:R]
    for j in range(1, nx):
        whole = whole * xown[j, 0:R]
    xinv[0:R] = 1.0 / (1.0 - whole)

    def begin(g, c, image, total):
        at = pl.ds(GL * g, GL)
        res[:, at] = image
        drn[:, at] = jnp.zeros(four, F32)
        sol[:, at] = jnp.zeros(four, F32)
        return c + jnp.sum(image * image, axis=(0, 1))

    rr_part = forth(0, zero[0:1], begin)
    rr_old = None
    for it in range(ITERS):
        beta_of = (lambda t: jnp.zeros_like(t)) if it == 0 else (lambda t, o=rr_old: t / o)

        def turn(g, c, total):
            at = pl.ds(GL * g, GL)
            new = res[:, at] + beta_of(total) * drn[:, at]
            drn[:, at] = new
            return c + jnp.sum(new * new, axis=(0, 1))

        y, dd, rr = back(2 * it + 1, rr_part, turn)
        if it > 0:
            y = y + beta_of(rr) * yold[...]
        yold[...] = y
        chunks = weigh(y)
        a_start(2 * it + 2, chunks)
        for k in range(nch):
            dd = dd + y[k] * chunks[k]

        def update(g, c, term, total):
            at = pl.ds(GL * g, GL)
            alpha = rr / total
            d = drn[:, at]
            sol[:, at] = sol[:, at] + alpha * d
            new = res[:, at] - alpha * (d + term)
            res[:, at] = new
            return c + jnp.sum(new * new, axis=(0, 1))

        rr_part = forth(2 * it + 2, dd, update)
        rr_old = rr


def on_device(nx, ny, rate_x, rate_y, land_mask, obs_cell, obs_count, innovation, obs_weight):
    lev, cx, cy = rate_x.shape
    slots = obs_cell.shape[2]
    nodes = nx * ny
    nch = nodes * slots // LANE
    assert (cx, cy) == (SUB, LANE) and lev % GL == 0 and (TR * lev) % nx == 0
    assert TR * lev <= LANE and LANE % slots == 0

    def plan(rate):
        decay = jnp.exp(-rate)
        one_minus = -jnp.expm1(-rate)
        scaling = jnp.sqrt(one_minus * (1.0 + decay))
        return decay, scaling * jnp.sqrt(jnp.sqrt(one_minus))

    dx, wx = plan(rate_x)
    dy, wy = plan(rate_y)
    occupied = (
        lax.broadcasted_iota(jnp.int32, (nodes, slots), 1) < obs_count[0][:, None]
    ).astype(F32)
    R = TR * lev // nx
    M = (2 * R + 1 + 7) // 8 * 8
    NXP = 2 * ITERS + 1
    field = (TR, lev, SUB, LANE)
    one = (lev, SUB, LANE)
    vm = pltpu.VMEM
    dma = pltpu.SemaphoreType.DMA
    Rp = (R + 7) // 8 * 8
    return pl.pallas_call(
        functools.partial(kernel, nx, ny, lev, slots),
        out_shape=(jax.ShapeDtypeStruct(field, F32),) * 2,
        in_specs=[pl.BlockSpec(memory_space=vm)] * 9,
        out_specs=(pl.BlockSpec(memory_space=vm),) * 2,
        scratch_shapes=[
            vm(field, F32), vm(field, F32),
            vm((TR * lev * SUB, LANE), F32), vm((TR * lev * SUB, LANE), F32),
            vm(field, F32),
            vm((3,) + one, F32), vm((3,) + one, F32), vm(one, F32), vm(one, F32),
            vm((7,) + one, F32), vm((7,) + one, F32), vm(one, F32), vm(one, F32),
            vm((TR * lev, LANE), F32), vm((TR * lev, LANE), F32),
            vm((TR * lev * SUB, nch * LANE), BF16), vm((LANE, nch * LANE), F32),
            vm((nch, 1, LANE), F32), vm((Rp, LANE), F32), vm((nx, M, LANE), F32),
            vm((NXP, nch, 1, LANE), F32), vm((NXP, nodes, 1, LANE), F32),
            vm((NXP + 1, nx, M, LANE), F32), vm((NXP + 1, nx, M, LANE), F32),
            vm((NXP, nx, M, LANE), F32), vm((NXP, nx, M, LANE), F32),
            vm((NXP + 1, 3 * SUB, LANE), F32), vm((NXP + 1, ny, 3 * SUB, LANE), F32),
            dma((NXP,)), dma((NXP,)), dma((NXP + 1,)), dma((NXP + 1,)),
            dma((NXP,)), dma((NXP,)), dma((NXP + 1,)), dma((NXP + 1,)),
        ],
        compiler_params=pltpu.CompilerParams(
            collective_id=0, has_side_effects=True, vmem_limit_bytes=56 * 1024 * 1024
        ),
    )(
        dx, wx, dy, wy, land_mask.astype(F32),
        obs_cell.reshape(nch, 1, LANE), occupied.reshape(nch, 1, LANE),
        innovation.reshape(nch, 1, LANE), obs_weight[0],
    )


def solution(mesh):
    placed = (
        P(None, "gx", "gy"),
        P(None, "gx", "gy"),
        P("gx", "gy"),
        P(("gx", "gy"), None, None),
        P(("gx", "gy"), None),
        P(("gx", "gy"), None, None),
        P(("gx", "gy"), None, None, None),
    )
    return jax.shard_map(
        functools.partial(on_device, mesh.shape["gx"], mesh.shape["gy"]),
        mesh=mesh,
        in_specs=placed,
        out_specs=(P(None, None, "gx", "gy"), P(None, None, "gx", "gy")),
        check_vma=False,
    )
```

time: 1610 us -> 146 us (0.09)
  waiting for transfers between devices: 670 us -> 0 us
  blocking collectives: 653 us -> 0 us
  Pallas kernels: 0 us -> 135 us
  other arithmetic: 135 us -> 5.25 us
  local copies, waits for them, and re-layouts: 102 us -> 4.67 us
  between operations: 22.1 us -> 0.66 us
    psum x10 -> x0, waiting for transfers between devices: 656 us -> none  [from_root(): return lax.psum(kept, axis)]
    all_gather x24 -> x0, blocking collectives: 511 us -> none  [entering_2(): gathered = jax.tree.map(lambda a: lax.all_gather(a, axis), part)]
    pallas_call x0 -> x1, Pallas kernels: none -> 135 us  [on_device(): pl.pallas_call(functools.partial(kernel, nx, ny, lev, slots), out_shape=(...]
    psum x3 -> x0, blocking collectives: 120 us -> none  [global_dot(): return lax.psum(jnp.sum(first_field * second_field), ('gx', 'gy'))]
    add x167 -> x0, other arithmetic: 66.5 us -> none  [the longest x50 41.4 us: compose_maps(): return (earlier[0] * following[0], following[0] * earlier[1] + following[1])]
    unnamed x285 -> x9, local copies, waits for them, and re-layouts: 33.8 us -> 3.01 us
    slice x107 -> x0, local copies, waits for them, and re-layouts: 22.5 us -> none  [the longest x10 8.1 us: shifted_next(): lax.slice_in_dim(back_offset, 1, line_length, axis=line_axis)]
    all_to_all x2 -> x0, blocking collectives: 21.7 us -> none  [on_device(): lax.all_to_all(picked, ('gx', 'gy'), split_axis=0, concat_axis=0, tiled=T...]
  transfers between devices with their start and end apart: 13 -> 0, of which waited for: 12 -> 0; matrix products, arithmetic and copies ran while one was open for 2% -> 0% of each run, Pallas kernels for 0% -> 0%
where the time goes in v1:
time: 146 us
  Pallas kernels  135 us (92%)
  other arithmetic  5.25 us (4%)
  local copies, waits for them, and re-layouts  4.67 us (3%)
    pallas_call x1, Pallas kernels, on_device(): pl.pallas_call(functools.partial(kernel, nx, ny, lev, slots), out_shape=(...  135 us
    unnamed x9, local copies, waits for them, and re-layouts  3.01 us

profile of v1, /device:TPU:0, one launch (start us, length us, event | category | flops | bytes accessed | tf_op | source)
XLA Modules:
  0.0 145.8 jit_solution(17306694919953952493)
XLA Ops:
  0.6 0.0 copy-start.1
  0.6 0.5 broadcast.28
  1.2 1.3 reduce.3
  2.5 0.1 iota.12
  2.6 0.0 copy-start.2
  2.6 0.1 lt.19
  2.6 1.3 convert_element_type.13.ocean_ref
  3.9 0.0 copy-done.1
  3.9 0.7 reshape.54.cell
  4.6 0.0 copy-done.2
  4.6 0.7 reshape.55.innov
  5.3 0.1 lt.20
  5.3 0.1 lt.21
  5.4 0.6 compare_convert_fusion.occ
  6.0 2.1 %sqrt_multiply_fusion = (f32[40,8,128]{2,1,0:T(8,128)}, f32[40,8,128]{2,1,0:T(8,128)}, f32[40,8,128]{2,1,0:T(8,128)}, f32[40,8,128]{2,1,0:T(8,128)}) fusion(f32[40,8,128]{2,1,0:T(8,128)} %param.8, f32[40,8,128]{2,1,0:T(8,128)} %param.7), kind=kLoop, calls=%fused_computation | loop fusion | flops 409600 | bytes 983040 | tf_op jit(solution)/shard_map/mul | solution.py:435
  8.1 135.2 %shard_map.86 = (f32[2,40,8,128]{3,2,1,0:T(8,128)}, f32[2,40,8,128]{3,2,1,0:T(8,128)}) custom-call(f32[40,8,128]{2,1,0:T(8,128)} %get-tuple-element.6.dx, f32[40,8,128]{2,1,0:T(8,128)} %get-tuple-element.7.wx, f32[40,8,128]{2,1,0:T(8,128)} %get-tuple-element.3.dy, f32[40,8,128]{2,1,0:T(8,128)} %get-tuple-element.2.wy, ...), custom_call_target="tpu_custom_call" | custom-call | tf_op jit(solution)/shard_map/pallas_call | solution.py:450
  143.3 0.0 copy-start
  143.3 1.8 %copy.11 = f32[2,40,8,128]{3,2,1,0:T(8,128)} copy(f32[2,40,8,128]{3,2,1,0:T(8,128)} %get-tuple-element.10) | data formatting | bytes 655360
  145.0 0.0 copy-done
  145.1 0.7 copy.12
  (1 shorter events, 0.0 us)
Async XLA Ops:
  0.6 3.3 %copy-start.1 = (s32[1,32,32]{2,1,0:T(8,128)S(1)}, s32[1,32,32]{2,1,0:T(8,128)}, u32[]{:S(2)}) copy-start(s32[1,32,32]{2,1,0:T(8,128)} %param.10) | copy-start | bytes 12292
  2.6 2.0 %copy-start.2 = (f32[1,32,32]{2,1,0:T(8,128)S(1)}, f32[1,32,32]{2,1,0:T(8,128)}, u32[]{:S(2)}) copy-start(f32[1,32,32]{2,1,0:T(8,128)} %param.12) | copy-start | bytes 12292
  143.3 1.8 %copy-start = (f32[2,40,8,128]{3,2,1,0:T(8,128)S(1)}, f32[2,40,8,128]{3,2,1,0:T(8,128)}, u32[]{:S(2)}) copy-start(f32[2,40,8,128]{3,2,1,0:T(8,128)} %get-tuple-element.11) | copy-start | bytes 983044

commit v2 on v1

v2 whole, which is shorter than its diff:
```python
import functools

import jax
import jax.numpy as jnp
from jax import lax
from jax.experimental import pallas as pl
from jax.experimental.pallas import tpu as pltpu
from jax.sharding import PartitionSpec as P

TR = 2
ITERS = 2
SUB = 8
LANE = 128
MESH = pl.DeviceIdType.MESH
F32 = jnp.float32
BF16 = jnp.bfloat16


def split3(a):
    hi = a.astype(BF16)
    rest = a - hi.astype(F32)
    mid = rest.astype(BF16)
    lo = (rest - mid.astype(F32)).astype(BF16)
    return hi, mid, lo


def kernel(
    nx, ny, lev, slots,
    rx, ry, mask_ref, cell, count, innov, wobs,
    sol, res,
    drn, v, ob, qb, cx, cy, tri,
    ex, xx, rows1h, lanes1h, occ, yold, xinv, xown,
    as_, ar, xs1, xr1, xs2, xr2, ys, yr,
    a_ss, a_rs, x1_ss, x1_rs, x2_ss, x2_rs, y_ss, y_rs,
):
    nodes = nx * ny
    per = LANE // slots
    nch = nodes * slots // LANE
    lines = TR * lev
    R = lines // nx
    mx = lax.axis_index("gx")
    my = lax.axis_index("gy")
    me = mx * ny + my
    NXP = 2 * ITERS + 1
    gxs = [lax.rem(mx + j, nx) for j in range(nx)]
    gys = [lax.rem(my + j, ny) for j in range(ny)]
    others = [(i, j) for i in range(nx) for j in range(ny) if i or j]

    barrier = pltpu.get_barrier_semaphore()
    for i, j in others:
        pl.semaphore_signal(barrier, inc=1, device_id=(gxs[i], gys[j]), device_id_type=MESH)

    one = (lev, SUB, LANE)
    four = (TR, lev, SUB, LANE)
    sub_i = lax.broadcasted_iota(jnp.int32, (SUB, LANE), 0)
    lane_i = lax.broadcasted_iota(jnp.int32, (SUB, LANE), 1)
    ocean = mask_ref[...].astype(F32)

    def sums_x(a, back):
        ax = a.ndim - 2
        for s in (1, 2, 4):
            if back:
                a = a + jnp.where(sub_i < SUB - s, pltpu.roll(a, SUB - s, ax), 0.0)
            else:
                a = a + jnp.where(sub_i >= s, pltpu.roll(a, s, ax), 0.0)
        return a

    def sums_x_after(a):
        b = sums_x(a, True)
        return b, jnp.where(sub_i < SUB - 1, pltpu.roll(b, SUB - 1, a.ndim - 2), 0.0)

    def sums_y(a, which):
        flat = a.reshape(a.size // LANE, LANE)
        lhs = jnp.concatenate(split3(flat), axis=1)
        return jnp.dot(lhs, tri[which], preferred_element_type=F32).reshape(a.shape)

    def shape_of(rate):
        decay = jnp.exp(-rate)
        series = 1.0
        for k in (9, 8, 7, 6, 5, 4, 3, 2):
            series = 1.0 - series * rate * (1.0 / k)
        one_minus = rate * series
        return jnp.sqrt(one_minus * (1.0 + decay)) * jnp.sqrt(jnp.sqrt(one_minus))

    def coefficients(co, w, c, end, after):
        p = jnp.exp(-c)
        pinv = jnp.exp(c)
        p2 = p * p
        total, later = after(p2)
        co[0] = w * pinv
        co[1] = p
        co[2] = w * p
        co[3] = p2
        co[4] = w * (p + pinv * later)
        co[5] = w * jnp.exp(c - end)
        return p, total

    def put_rows(ref, a):
        ref[...] = a.reshape(lines * SUB, LANE)

    def local_x(u):
        s = sums_x(u * cx[0], False)
        total, later = sums_x_after(s * cx[3])
        v[...] = cx[2] * s + cx[0] * later
        put_rows(ob, cx[1] * s)
        put_rows(qb, total)

    tag = (
        lax.broadcasted_iota(jnp.int32, four, 3)
        - lax.broadcasted_iota(jnp.int32, four, 0) * lev
        - lax.broadcasted_iota(jnp.int32, four, 1)
    )

    def pick(a, col):
        column = jnp.broadcast_to(a[..., col : col + 1], four)
        return jnp.sum(jnp.where(tag == 0, column, 0.0), axis=(0, 1))

    def local_y(u):
        s = sums_y(u * cy[0], 0)
        m = s * cy[3]
        later = sums_y(m, 1)
        v[...] = cy[2] * s + cy[0] * later
        return pick(cy[1] * s, LANE - 1), pick(later + m, 0)

    def after_x():
        def rows(ref):
            return ref[...].reshape(TR, lev, 1, LANE)

        return v[...] + cx[4] * rows(ex) + cx[5] * rows(xx)

    def after_y(e, x):
        def columns(a):
            parts = [jnp.broadcast_to(a[:, t : t + 1], (SUB, LANE)) for t in range(lines)]
            return jnp.stack(parts).reshape(four)

        return v[...] + cy[4] * columns(e) + cy[5] * columns(x)

    zero = jnp.zeros((SUB, LANE), F32)
    zero_row = jnp.zeros((1, LANE), F32)

    def wait_all(buf, sem):
        pltpu.make_async_copy(buf, buf, sem).wait()

    def x_start(src, dst, ss, rs, p):
        for i in range(1, nx):
            pltpu.make_async_remote_copy(
                src_ref=src.at[p, gxs[i]], dst_ref=dst.at[p, mx], send_sem=ss.at[p], recv_sem=rs.at[p],
                device_id=(gxs[i], my), device_id_type=MESH,
            ).start()
        dst[p, mx] = src[p, mx]

    def x_wait(src, dst, ss, rs, p):
        wait_all(dst.at[p, pl.ds(0, nx - 1)], rs.at[p])
        wait_all(src.at[p, pl.ds(0, nx - 1)], ss.at[p])

    def x_fill(p, row):
        for j in range(nx):
            xs1[p, j, 0:R] = ob[pl.ds(SUB - 1 + SUB * R * j, R, stride=SUB), :]
            xs1[p, j, R : 2 * R] = qb[pl.ds(SUB * R * j, R, stride=SUB), :]
            xs1[p, j, 2 * R : 2 * R + 1] = row

    def x_exchange(p, row):
        x_fill(p, row)
        x_start(xs1, xr1, x1_ss, x1_rs, p)
        x_wait(xs1, xr1, x1_ss, x1_rs, p)
        A = [xown[j, 0:R] for j in range(nx)]
        C = [xown[j, R : 2 * R] for j in range(nx)]
        F = [xr1[p, j, 0:R] for j in range(nx)]
        B = [xr1[p, j, R : 2 * R] for j in range(nx)]
        inv = xinv[0:R]
        e = F[0]
        for j in range(1, nx):
            e = F[j] + A[j] * e
        e = e * inv
        gs = []
        for j in range(nx):
            xs2[p, j, 0:R] = e
            gs.append(B[j] + C[j] * e)
            e = F[j] + A[j] * e
        x = gs[nx - 1]
        for j in range(nx - 2, -1, -1):
            x = gs[j] + A[j] * x
        x = x * inv
        for j in range(nx - 1, -1, -1):
            xs2[p, j, R : 2 * R] = x
            x = gs[j] + A[j] * x
        x_start(xs2, xr2, x2_ss, x2_rs, p)
        total = xr1[p, 0, 2 * R : 2 * R + 1]
        for j in range(1, nx):
            total = total + xr1[p, j, 2 * R : 2 * R + 1]
        x_wait(xs2, xr2, x2_ss, x2_rs, p)
        for j in range(nx):
            ex[R * j : R * (j + 1)] = xr2[p, j, 0:R]
            xx[R * j : R * (j + 1)] = xr2[p, j, R : 2 * R]
        return total

    def y_start(p, f, b, row):
        ys[p, 0:SUB] = f
        ys[p, SUB : 2 * SUB] = b
        ys[p, 2 * SUB : 3 * SUB] = jnp.broadcast_to(row, (SUB, LANE))
        for j in range(1, ny):
            pltpu.make_async_remote_copy(
                src_ref=ys.at[p], dst_ref=yr.at[p, my], send_sem=y_ss.at[p], recv_sem=y_rs.at[p],
                device_id=(mx, gys[j]), device_id_type=MESH,
            ).start()
        yr[p, my] = ys[p]

    def y_wait(p):
        wait_all(yr.at[p, pl.ds(0, ny - 1)], y_rs.at[p])
        wait_all(yr.at[p, pl.ds(0, ny - 1)], y_ss.at[p])

    def y_exchange(p, f, b, row):
        y_start(p, f, b, row)
        y_wait(p)
        total = yr[p, 0, 2 * SUB : 2 * SUB + 1]
        for j in range(1, ny):
            total = total + yr[p, j, 2 * SUB : 2 * SUB + 1]
        e, mine_e, gs = zero, zero, []
        for j in range(ny):
            mine_e = jnp.where(my == j, e, mine_e)
            gs.append(yr[p, j, SUB : 2 * SUB] + yr[NXP, j, SUB : 2 * SUB] * e)
            e = yr[p, j, 0:SUB] + yr[NXP, j, 0:SUB] * e
        x, mine_x = zero, zero
        for j in range(ny - 1, -1, -1):
            mine_x = jnp.where(my == j, x, mine_x)
            x = gs[j] + yr[NXP, j, 0:SUB] * x
        return mine_e, mine_x, total

    def a_start(p, chunks):
        for c in range(nch):
            as_[p, c] = chunks[c]
        for i, j in others:
            pltpu.make_async_remote_copy(
                src_ref=as_.at[p, (gxs[i] * ny + gys[j]) // per], dst_ref=ar.at[p, me],
                send_sem=a_ss.at[p], recv_sem=a_rs.at[p],
                device_id=(gxs[i], gys[j]), device_id_type=MESH,
            ).start()
        ar[p, me] = as_[p, me // per]

    def a_wait(p):
        wait_all(ar.at[p, pl.ds(0, nodes - 1)], a_rs.at[p])
        wait_all(ar.at[p, pl.ds(0, nodes - 1)], a_ss.at[p])
        got = ar[p].reshape(nch, per, 1, LANE)
        block = lax.broadcasted_iota(jnp.int32, (nch, 1, LANE), 2) // slots
        mine = lax.rem(me, per)
        total = jnp.zeros((nch, 1, LANE), F32)
        for i in range(per):
            turned = pltpu.roll(got[:, i], lax.rem(i - mine + per, per) * slots, 2)
            total = jnp.where(block == i, turned, total)
        return total

    def line_up(ref, c):
        return jnp.concatenate([ref[0, per * c + i : per * c + i + 1, :] for i in range(per)], axis=1)

    def weigh(y):
        per_block = wobs.shape[2] // LANE
        chunks = []
        for n in range(wobs.shape[1]):
            row = jnp.concatenate([y[per_block * n + a] * occ[per_block * n + a] for a in range(per_block)], axis=1)
            z = lax.dot_general(
                jnp.broadcast_to(row, (SUB, row.shape[1])), wobs[0, n], (((1,), (1,)), ((), ())),
                precision=lax.Precision.HIGHEST, preferred_element_type=F32,
            )
            for a in range(per_block):
                chunks.append(z[0:1, a * LANE : (a + 1) * LANE] * occ[per_block * n + a])
        return chunks

    def onehots():
        ri = lax.broadcasted_iota(jnp.int32, (lines * SUB, LANE), 0)
        li = lax.broadcasted_iota(jnp.int32, (LANE, LANE), 0)
        for c in range(nch):
            here = line_up(cell, c)
            cols = slice(c * LANE, (c + 1) * LANE)
            rows1h[:, cols] = jnp.where(ri == here // LANE, 1.0, 0.0).astype(BF16)
            lanes1h[:, cols] = jnp.where(li == lax.rem(here, LANE), 1.0, 0.0)

    def observe(field):
        t = jnp.transpose(field.reshape(lines * SUB, LANE))
        lhs = jnp.concatenate(split3(t), axis=0)
        chunks = []
        for c in range(0, nch, 2):
            wide = min(2, nch - c)
            cols = slice(c * LANE, (c + wide) * LANE)
            got = jnp.dot(lhs, rows1h[:, cols], preferred_element_type=F32)
            got = (got[0:LANE] + got[LANE : 2 * LANE]) + got[2 * LANE :]
            got = jnp.sum(got * lanes1h[:, cols], axis=0, keepdims=True)
            chunks += [got[:, k * LANE : (k + 1) * LANE] for k in range(wide)]
        return chunks

    def deposit(vals):
        row = jnp.concatenate([vals[c] for c in range(nch)], axis=1)
        spread = lanes1h[...]
        rhs = jnp.concatenate([(spread * part.astype(F32)).astype(BF16) for part in split3(row)], axis=0)
        got = lax.dot_general(rows1h[...], rhs, (((1,), (1,)), ((), ())), preferred_element_type=F32)
        got = (got[:, 0:LANE] + got[:, LANE : 2 * LANE]) + got[:, 2 * LANE :]
        return got.reshape(four)

    def lane_total(row):
        return jnp.broadcast_to(jnp.sum(row, axis=1, keepdims=True), (1, LANE))

    def inner(a, b):
        return jnp.sum(jnp.sum(a * b, axis=(0, 1)), axis=0, keepdims=True)

    def forth(p, row):
        f, b = local_y(ocean * deposit(a_wait(p)))
        e, x, total = y_exchange(p, f, b, row)
        local_x(after_y(e, x))
        total = lane_total(x_exchange(p, total))
        return ocean * after_x(), total

    def back(p, row):
        local_x(ocean * res[...])
        total = x_exchange(p, row)
        f, b = local_y(after_x())
        e, x, total = y_exchange(p, f, b, total)
        a_start(p, observe(ocean * after_y(e, x)))
        return lane_total(total)

    for buf in (xs1, xs2):
        buf[...] = jnp.zeros(buf.shape, F32)
    block = lax.broadcasted_iota(jnp.int32, (1, LANE), 1) // slots
    place = lax.rem(lax.broadcasted_iota(jnp.int32, (1, LANE), 1), slots)
    for c in range(nch):
        held = jnp.zeros((1, LANE), jnp.int32)
        for i in range(per):
            held = jnp.where(block == i, count[:, per * c + i : per * c + i + 1], held)
        occ[c] = jnp.where(place < held, 1.0, 0.0)
    chunks = weigh([line_up(innov, c) for c in range(nch)])
    pl.semaphore_wait(barrier, nodes - 1)
    a_start(0, chunks)

    ti = lax.broadcasted_iota(jnp.int32, (LANE, LANE), 0)
    tj = lax.broadcasted_iota(jnp.int32, (LANE, LANE), 1)
    for k in range(3):
        tri[0, k * LANE : (k + 1) * LANE] = jnp.where(ti <= tj, 1.0, 0.0).astype(BF16)
        tri[1, k * LANE : (k + 1) * LANE] = jnp.where(ti > tj, 1.0, 0.0).astype(BF16)

    rate = rx[...]
    c = sums_x(rate, False)
    p, b = coefficients(cx, shape_of(rate), c, c[:, SUB - 1 :, :], sums_x_after)
    put_rows(ob, jnp.stack([p] * TR))
    put_rows(qb, jnp.stack([b] * TR))
    x_fill(NXP, zero_row)
    x_start(xs1, xr1, x1_ss, x1_rs, NXP)

    def after(a):
        later = sums_y(a, 1)
        return later + a, later

    rate = ry[...]
    c = sums_y(rate, 0)
    p, b = coefficients(cy, shape_of(rate), c, c[:, :, LANE - 1 :], after)
    p = jnp.broadcast_to(p[None], four)
    b = jnp.broadcast_to(b[None], four)
    y_start(NXP, pick(p, LANE - 1), pick(b, 0), zero_row)
    onehots()
    y_wait(NXP)
    x_wait(xs1, xr1, x1_ss, x1_rs, NXP)
    xown[...] = xr1[NXP]
    whole = xown[0, 0:R]
    for j in range(1, nx):
        whole = whole * xown[j, 0:R]
    xinv[0:R] = 1.0 / (1.0 - whole)

    right, _ = forth(0, zero_row)
    res[...] = right
    rr_part = inner(right, right)
    rr = None
    for it in range(ITERS):
        rr_old = rr
        rr = back(2 * it + 1, rr_part)
        if it == 0:
            direction = res[...]
        else:
            direction = res[...] + (rr / rr_old) * drn[...]
        drn[...] = direction
        dd = inner(direction, direction)
        y = a_wait(2 * it + 1)
        if it > 0:
            y = y + (rr / rr_old) * yold[...]
        yold[...] = y
        chunks = weigh(y)
        a_start(2 * it + 2, chunks)
        for k in range(nch):
            dd = dd + y[k] * chunks[k]
        term, total = forth(2 * it + 2, dd)
        alpha = rr / total
        direction = drn[...]
        sol[...] = alpha * direction if it == 0 else sol[...] + alpha * direction
        new = res[...] - alpha * (direction + term)
        res[...] = new
        if it < ITERS - 1:
            rr_part = inner(new, new)


def on_device(nx, ny, rate_x, rate_y, land_mask, obs_cell, obs_count, innovation, obs_weight):
    lev, sx, sy = rate_x.shape
    slots = obs_cell.shape[2]
    nodes = nx * ny
    nch = nodes * slots // LANE
    lines = TR * lev
    assert (sx, sy) == (SUB, LANE) and lines % nx == 0 and lines <= LANE and LANE % slots == 0
    R = lines // nx
    M = (2 * R + 1 + 7) // 8 * 8
    NXP = 2 * ITERS + 1
    field = (TR, lev, SUB, LANE)
    one = (lev, SUB, LANE)
    vm = pltpu.VMEM
    dma = pltpu.SemaphoreType.DMA
    Rp = (R + 7) // 8 * 8
    return pl.pallas_call(
        functools.partial(kernel, nx, ny, lev, slots),
        out_shape=(jax.ShapeDtypeStruct(field, F32),) * 2,
        in_specs=[pl.BlockSpec(memory_space=vm)] * 7,
        out_specs=(pl.BlockSpec(memory_space=vm),) * 2,
        scratch_shapes=[
            vm(field, F32), vm(field, F32),
            vm((lines * SUB, LANE), F32), vm((lines * SUB, LANE), F32),
            vm((6,) + one, F32), vm((6,) + one, F32), vm((2, 3 * LANE, LANE), BF16),
            vm((lines, LANE), F32), vm((lines, LANE), F32),
            vm((lines * SUB, nch * LANE), BF16), vm((LANE, nch * LANE), F32),
            vm((nch, 1, LANE), F32), vm((nch, 1, LANE), F32),
            vm((Rp, LANE), F32), vm((nx, M, LANE), F32),
            vm((NXP, nch, 1, LANE), F32), vm((NXP, nodes, 1, LANE), F32),
            vm((NXP + 1, nx, M, LANE), F32), vm((NXP + 1, nx, M, LANE), F32),
            vm((NXP, nx, M, LANE), F32), vm((NXP, nx, M, LANE), F32),
            vm((NXP + 1, 3 * SUB, LANE), F32), vm((NXP + 1, ny, 3 * SUB, LANE), F32),
            dma((NXP,)), dma((NXP,)), dma((NXP + 1,)), dma((NXP + 1,)),
            dma((NXP,)), dma((NXP,)), dma((NXP + 1,)), dma((NXP + 1,)),
        ],
        compiler_params=pltpu.CompilerParams(
            collective_id=0, has_side_effects=True, vmem_limit_bytes=56 * 1024 * 1024
        ),
    )(rate_x, rate_y, land_mask, obs_cell, obs_count, innovation, obs_weight)


def solution(mesh):
    placed = (
        P(None, "gx", "gy"),
        P(None, "gx", "gy"),
        P("gx", "gy"),
        P(("gx", "gy"), None, None),
        P(("gx", "gy"), None),
        P(("gx", "gy"), None, None),
        P(("gx", "gy"), None, None, None),
    )
    return jax.shard_map(
        functools.partial(on_device, mesh.shape["gx"], mesh.shape["gy"]),
        mesh=mesh,
        in_specs=placed,
        out_specs=(P(None, None, "gx", "gy"), P(None, None, "gx", "gy")),
        check_vma=False,
    )
```

time: 146 us -> 106 us (0.73)
  Pallas kernels: 135 us -> 103 us
  other arithmetic: 5.25 us -> 0 us
  local copies, waits for them, and re-layouts: 4.67 us -> 2.49 us
    pallas_call x1, Pallas kernels: 135 us -> 103 us  [on_device(): pl.pallas_call(functools.partial(kernel, nx, ny, lev, slots), out_shape=(...]
    mul x1 -> x0, other arithmetic: 2.05 us -> none  [plan(): return (decay, scaling * jnp.sqrt(jnp.sqrt(one_minus)))]
    convert_element_type x2 -> x0, other arithmetic: 1.88 us -> none  [the longest x1 1.28 us: on_device(): land_mask.astype(F32)]
    unnamed x9 -> x4, local copies, waits for them, and re-layouts: 3.01 us -> 2.49 us
where the time goes in v2:
time: 106 us
  Pallas kernels  103 us (97%)
  local copies, waits for them, and re-layouts  2.49 us (2%)
    pallas_call x1, Pallas kernels, on_device(): pl.pallas_call(functools.partial(kernel, nx, ny, lev, slots), out_shape=(...  103 us
    unnamed x4, local copies, waits for them, and re-layouts  2.49 us

profile of v2, /device:TPU:0, one launch (start us, length us, event | category | flops | bytes accessed | tf_op | source)
XLA Modules:
  0.0 105.8 jit_solution(14627593251953229455)
XLA Ops:
  0.6 102.6 %shard_map.86 = (f32[2,40,8,128]{3,2,1,0:T(8,128)}, f32[2,40,8,128]{3,2,1,0:T(8,128)}) custom-call(f32[40,8,128]{2,1,0:T(8,128)} %rx.1, f32[40,8,128]{2,1,0:T(8,128)} %ry.1, s32[8,128]{1,0:T(8,128)} %mask_ref.1, s32[1,32,32]{2,1,0:T(8,128)} %cell.1, s32[1,32]{1,0:T(1,128)} %count.1, f32[1,32,32]{2,1,0:T(8,128)} %innov.1, f32[1,4,256,256]{3,2,1,0:T(8,128)} %wobs.1), custom_call_target="tpu_custom_call" | custom-call | tf_op jit(solution)/shard_map/pallas_call | solution.py:411
  103.3 0.0 copy-start
  103.3 1.8 %copy.11 = f32[2,40,8,128]{3,2,1,0:T(8,128)} copy(f32[2,40,8,128]{3,2,1,0:T(8,128)} %get-tuple-element.4) | data formatting | bytes 655360
  105.0 0.0 copy-done
  105.0 0.7 copy.12
Async XLA Ops:
  103.3 1.8 %copy-start = (f32[2,40,8,128]{3,2,1,0:T(8,128)S(1)}, f32[2,40,8,128]{3,2,1,0:T(8,128)}, u32[]{:S(2)}) copy-start(f32[2,40,8,128]{3,2,1,0:T(8,128)} %get-tuple-element.5) | copy-start | bytes 983044

commit v3 on v2

v3 whole, which is shorter than its diff:
```python
import functools

import jax
import jax.numpy as jnp
from jax import lax
from jax.experimental import pallas as pl
from jax.experimental.pallas import tpu as pltpu
from jax.sharding import PartitionSpec as P

TR = 2
ITERS = 2
SUB = 8
LANE = 128
MESH = pl.DeviceIdType.MESH
F32 = jnp.float32
BF16 = jnp.bfloat16


HALF = LANE // 2


def stages(lines):
    first = lines * 3 // 5
    return ((0, first), (first, lines))


def x_message(rows, scalar):
    return (2 * rows + scalar + SUB - 1) // SUB * SUB


def split3(a):
    hi = a.astype(BF16)
    rest = a - hi.astype(F32)
    mid = rest.astype(BF16)
    lo = (rest - mid.astype(F32)).astype(BF16)
    return hi, mid, lo


def kernel(
    nx, ny, lev, slots,
    rx, ry, mask_ref, cell, count, innov, wobs,
    sol, res,
    drn, v, ob, qb, cx, cy, tri, w3,
    ex, xx, rows1h, lanes1h, occ, yold, xinv,
    as_, ar, xs1, xr1, xs2, xr2, ys, yr,
    a_ss, a_rs, x1_ss, x1_rs, x2_ss, x2_rs, y_ss, y_rs,
):
    nodes = nx * ny
    per = LANE // slots
    nch = nodes * slots // LANE
    lines = TR * lev
    bounds = stages(lines)
    NS = len(bounds)
    mx = lax.axis_index("gx")
    my = lax.axis_index("gy")
    me = mx * ny + my
    NXP = 2 * ITERS + 1
    gxs = [lax.rem(mx + j, nx) for j in range(nx)]
    gys = [lax.rem(my + j, ny) for j in range(ny)]
    others = [(i, j) for i in range(nx) for j in range(ny) if i or j]

    barrier = pltpu.get_barrier_semaphore()
    for i, j in others:
        pl.semaphore_signal(barrier, inc=1, device_id=(gxs[i], gys[j]), device_id_type=MESH)

    three = (lines, SUB, LANE)
    sub_i = lax.broadcasted_iota(jnp.int32, (SUB, LANE), 0)
    lane_i = lax.broadcasted_iota(jnp.int32, (SUB, LANE), 1)
    ocean = mask_ref[...].astype(F32)

    def sums_x(a, back):
        ax = a.ndim - 2
        for s in (1, 2, 4):
            if back:
                a = a + jnp.where(sub_i < SUB - s, pltpu.roll(a, SUB - s, ax), 0.0)
            else:
                a = a + jnp.where(sub_i >= s, pltpu.roll(a, s, ax), 0.0)
        return a

    def sums_x_after(a):
        b = sums_x(a, True)
        return b, jnp.where(sub_i < SUB - 1, pltpu.roll(b, SUB - 1, a.ndim - 2), 0.0)

    def sums_y(a, which):
        flat = a.reshape(a.size // LANE, LANE)
        lhs = jnp.concatenate(split3(flat), axis=1)
        return jnp.dot(lhs, tri[which], preferred_element_type=F32).reshape(a.shape)

    def shape_of(rate):
        decay = jnp.exp(-rate)
        series = 1.0
        for k in (9, 8, 7, 6, 5, 4, 3, 2):
            series = 1.0 - series * rate * (1.0 / k)
        one_minus = rate * series
        return jnp.sqrt(one_minus * (1.0 + decay)) * jnp.sqrt(jnp.sqrt(one_minus))

    def coefficients(co, w, c, end, after):
        p = jnp.exp(-c)
        pinv = jnp.exp(c)
        p2 = p * p
        total, later = after(p2)
        co[0] = w * pinv
        co[1] = p
        co[2] = w * p
        co[3] = p2
        co[4] = w * (p + pinv * later)
        co[5] = w * jnp.exp(c - end)
        return p, total

    def put_rows(ref, a, s):
        t0, t1 = bounds[s]
        ref[t0 * SUB : t1 * SUB] = a.reshape((t1 - t0) * SUB, LANE)

    def of_lines(a, s):
        t0, t1 = bounds[s]
        parts = []
        while t0 < t1:
            low = t0 % lev
            n = min(t1 - t0, lev - low)
            parts.append(a[low : low + n])
            t0 += n
        return parts[0] if len(parts) == 1 else jnp.concatenate(parts, axis=0)

    def local_x(u, s):
        cs = [of_lines(cx[k], s) for k in range(4)]
        f = sums_x(u * cs[0], False)
        total, later = sums_x_after(f * cs[3])
        v[bounds[s][0] : bounds[s][1]] = cs[2] * f + cs[0] * later
        put_rows(ob, cs[1] * f, s)
        put_rows(qb, total, s)

    def pick(a, col, s, shift):
        n = bounds[s][1] - bounds[s][0]
        tag = lax.broadcasted_iota(jnp.int32, (n, SUB, LANE), 2) - lax.broadcasted_iota(jnp.int32, (n, SUB, LANE), 0)
        column = jnp.broadcast_to(a[..., col : col + 1], a.shape)
        return jnp.sum(jnp.where(tag == shift, column, 0.0), axis=0)

    def local_y(u, s):
        cs = [of_lines(cy[k], s) for k in range(4)]
        f = sums_y(u * cs[0], 0)
        m = f * cs[3]
        later = sums_y(m, 1)
        v[bounds[s][0] : bounds[s][1]] = cs[2] * f + cs[0] * later
        return pick(cs[1] * f, LANE - 1, s, 0) + pick(later + m, 0, s, HALF)

    def after_x(s):
        t0, t1 = bounds[s]

        def rows(ref):
            return ref[t0:t1].reshape(t1 - t0, 1, LANE)

        return v[t0:t1] + of_lines(cx[4], s) * rows(ex) + of_lines(cx[5], s) * rows(xx)

    def after_y(e, x, s):
        t0, t1 = bounds[s]

        def columns(a):
            return jnp.stack([jnp.broadcast_to(a[:, t : t + 1], (SUB, LANE)) for t in range(t1 - t0)])

        return v[t0:t1] + of_lines(cy[4], s) * columns(e) + of_lines(cy[5], s) * columns(x)

    zero = jnp.zeros((SUB, LANE), F32)
    zero_row = jnp.zeros((1, LANE), F32)

    def wait_all(buf, sem):
        pltpu.make_async_copy(buf, buf, sem).wait()

    def x_rows(s):
        r = (bounds[s][1] - bounds[s][0]) // nx
        return r, x_message(r, s == 0)

    def x_copies(src, dst, ss, rs, q, s):
        m = x_rows(s)[1]
        for i in range(1, nx):
            pltpu.make_async_remote_copy(
                src_ref=src.at[q, gxs[i], pl.ds(0, m)], dst_ref=dst.at[q, mx, pl.ds(0, m)],
                send_sem=ss.at[q], recv_sem=rs.at[q],
                device_id=(gxs[i], my), device_id_type=MESH,
            ).start()
        dst[q, mx] = src[q, mx]

    def x_wait(dst, ss, rs, q, s):
        m = x_rows(s)[1]
        wait_all(dst.at[q, pl.ds(0, nx - 1), pl.ds(0, m)], rs.at[q])
        wait_all(dst.at[q, pl.ds(0, nx - 1), pl.ds(0, m)], ss.at[q])

    def x_send(p, s, row=None):
        q = NS * p + s
        r = x_rows(s)[0]
        t0 = bounds[s][0]
        for j in range(nx):
            xs1[q, j, 0:r] = ob[pl.ds(SUB - 1 + SUB * (t0 + r * j), r, stride=SUB), :]
            xs1[q, j, r : 2 * r] = qb[pl.ds(SUB * (t0 + r * j), r, stride=SUB), :]
            if row is not None:
                xs1[q, j, 2 * r : 2 * r + 1] = row
        x_copies(xs1, xr1, x1_ss, x1_rs, q, s)

    def x_solve(p, s):
        q = NS * p + s
        k = NS * NXP + s
        r = x_rows(s)[0]
        x_wait(xr1, x1_ss, x1_rs, q, s)
        A = [xr1[k, j, 0:r] for j in range(nx)]
        C = [xr1[k, j, r : 2 * r] for j in range(nx)]
        F = [xr1[q, j, 0:r] for j in range(nx)]
        B = [xr1[q, j, r : 2 * r] for j in range(nx)]
        inv = xinv[s, 0:r]
        e = F[0]
        for j in range(1, nx):
            e = F[j] + A[j] * e
        e = e * inv
        gs = []
        for j in range(nx):
            xs2[q, j, 0:r] = e
            gs.append(B[j] + C[j] * e)
            e = F[j] + A[j] * e
        x = gs[nx - 1]
        for j in range(nx - 2, -1, -1):
            x = gs[j] + A[j] * x
        x = x * inv
        for j in range(nx - 1, -1, -1):
            xs2[q, j, r : 2 * r] = x
            x = gs[j] + A[j] * x
        x_copies(xs2, xr2, x2_ss, x2_rs, q, s)
        if s == 0:
            total = xr1[q, 0, 2 * r : 2 * r + 1]
            for j in range(1, nx):
                total = total + xr1[q, j, 2 * r : 2 * r + 1]
            return total

    def x_finish(p, s):
        q = NS * p + s
        r = x_rows(s)[0]
        t0 = bounds[s][0]
        x_wait(xr2, x2_ss, x2_rs, q, s)
        for j in range(nx):
            ex[t0 + r * j : t0 + r * (j + 1)] = xr2[q, j, 0:r]
            xx[t0 + r * j : t0 + r * (j + 1)] = xr2[q, j, r : 2 * r]

    def y_send(p, s, tile, total=None):
        q = NS * p + s
        if total is not None:
            tile = jnp.where(lane_i == LANE - 1, total, tile)
        ys[q] = tile
        for j in range(1, ny):
            pltpu.make_async_remote_copy(
                src_ref=ys.at[q], dst_ref=yr.at[q, my], send_sem=y_ss.at[q], recv_sem=y_rs.at[q],
                device_id=(mx, gys[j]), device_id_type=MESH,
            ).start()
        yr[q, my] = tile

    def y_wait(q):
        wait_all(yr.at[q, pl.ds(0, ny - 1)], y_rs.at[q])
        wait_all(yr.at[q, pl.ds(0, ny - 1)], y_ss.at[q])

    def y_finish(p, s):
        q = NS * p + s
        k = NS * NXP + s
        y_wait(q)
        tiles = [yr[q, j] for j in range(ny)]
        keeps = [yr[k, j] for j in range(ny)]
        e, mine_e, gs = zero, zero, []
        for j in range(ny):
            mine_e = jnp.where(my == j, e, mine_e)
            gs.append(pltpu.roll(tiles[j], HALF, 1) + pltpu.roll(keeps[j], HALF, 1) * e)
            e = tiles[j] + keeps[j] * e
        x, mine_x = zero, zero
        for j in range(ny - 1, -1, -1):
            mine_x = jnp.where(my == j, x, mine_x)
            x = gs[j] + keeps[j] * x
        total = tiles[0]
        for j in range(1, ny):
            total = total + tiles[j]
        return mine_e, mine_x, jnp.broadcast_to(total[0:1, LANE - 1 : LANE], (1, LANE))

    def a_start(p, chunks):
        for c in range(nch):
            as_[p, c] = chunks[c]
        for i, j in others:
            pltpu.make_async_remote_copy(
                src_ref=as_.at[p, (gxs[i] * ny + gys[j]) // per], dst_ref=ar.at[p, me],
                send_sem=a_ss.at[p], recv_sem=a_rs.at[p],
                device_id=(gxs[i], gys[j]), device_id_type=MESH,
            ).start()
        ar[p, me] = as_[p, me // per]

    def a_wait(p):
        wait_all(ar.at[p, pl.ds(0, nodes - 1)], a_rs.at[p])
        wait_all(ar.at[p, pl.ds(0, nodes - 1)], a_ss.at[p])
        got = ar[p].reshape(nch, per, 1, LANE)
        block = lax.broadcasted_iota(jnp.int32, (nch, 1, LANE), 2) // slots
        mine = lax.rem(me, per)
        total = jnp.zeros((nch, 1, LANE), F32)
        for i in range(per):
            turned = pltpu.roll(got[:, i], lax.rem(i - mine + per, per) * slots, 2)
            total = jnp.where(block == i, turned, total)
        return total

    def line_up(ref, c):
        return jnp.concatenate([ref[0, per * c + i : per * c + i + 1, :] for i in range(per)], axis=1)

    def weigh(y):
        per_block = wobs.shape[2] // LANE
        chunks = []
        for n in range(wobs.shape[1]):
            row = jnp.concatenate([y[per_block * n + a] * occ[per_block * n + a] for a in range(per_block)], axis=1)
            which = lax.broadcasted_iota(jnp.int32, (2 * SUB, row.shape[1]), 0)
            lhs = jnp.zeros(which.shape, F32)
            for k, part in enumerate(split3(row)):
                lhs = jnp.where(which == k, part.astype(F32), lhs)
            lhs = lhs.astype(BF16)
            z = jnp.dot(lhs, w3[n, 2], preferred_element_type=F32)
            z = z + jnp.dot(lhs, w3[n, 1], preferred_element_type=F32)
            z = z + jnp.dot(lhs, w3[n, 0], preferred_element_type=F32)
            z = jnp.sum(z, axis=0, keepdims=True)
            for a in range(per_block):
                chunks.append(z[0:1, a * LANE : (a + 1) * LANE] * occ[per_block * n + a])
        return chunks

    def onehots():
        ri = lax.broadcasted_iota(jnp.int32, (lines * SUB, LANE), 0)
        li = lax.broadcasted_iota(jnp.int32, (LANE, LANE), 0)
        for c in range(nch):
            here = line_up(cell, c)
            cols = slice(c * LANE, (c + 1) * LANE)
            rows1h[:, cols] = jnp.where(ri == here // LANE, 1.0, 0.0).astype(BF16)
            lanes1h[:, cols] = jnp.where(li == lax.rem(here, LANE), 1.0, 0.0)

    def observe(field):
        t = jnp.transpose(field.reshape(lines * SUB, LANE))
        lhs = jnp.concatenate(split3(t), axis=0)
        chunks = []
        for c in range(0, nch, 2):
            wide = min(2, nch - c)
            cols = slice(c * LANE, (c + wide) * LANE)
            got = jnp.dot(lhs, rows1h[:, cols], preferred_element_type=F32)
            got = (got[0:LANE] + got[LANE : 2 * LANE]) + got[2 * LANE :]
            got = jnp.sum(got * lanes1h[:, cols], axis=0, keepdims=True)
            chunks += [got[:, k * LANE : (k + 1) * LANE] for k in range(wide)]
        return chunks

    def deposit(vals):
        row = jnp.concatenate([vals[c] for c in range(nch)], axis=1)
        spread = lanes1h[...]
        rhs = jnp.concatenate([(spread * part.astype(F32)).astype(BF16) for part in split3(row)], axis=0)
        got = lax.dot_general(rows1h[...], rhs, (((1,), (1,)), ((), ())), preferred_element_type=F32)
        got = (got[:, 0:LANE] + got[:, LANE : 2 * LANE]) + got[:, 2 * LANE :]
        return got.reshape(three)

    def lane_total(row):
        return jnp.broadcast_to(jnp.sum(row, axis=1, keepdims=True), (1, LANE))

    def inner(a, b):
        return jnp.sum(jnp.sum(a * b, axis=0), axis=0, keepdims=True)

    every = range(NS)

    def part(ref, s):
        return ref.at[bounds[s][0] : bounds[s][1]]

    def forth_y(p, row):
        field = deposit(a_wait(p))
        for s in every:
            tile = local_y(ocean * field[bounds[s][0] : bounds[s][1]], s)
            y_send(p, s, tile, lane_total(row) if s == 0 else None)

    def forth_x(p):
        total = None
        for s in every:
            e, x, t = y_finish(p, s)
            local_x(after_y(e, x, s), s)
            x_send(p, s, t if s == 0 else None)
        for s in every:
            t = x_solve(p, s)
            total = t if s == 0 else total
        return total

    def back(p, row, beside):
        for s in every:
            local_x(ocean * part(res, s)[...], s)
            x_send(p, s, row if s == 0 else None)
        beside()
        total = None
        for s in every:
            t = x_solve(p, s)
            total = lane_total(t) if s == 0 else total
        for s in every:
            x_finish(p, s)
            y_send(p, s, local_y(after_x(s), s), total if s == 0 else None)
        fields = []
        for s in every:
            e, x, t = y_finish(p, s)
            fields.append(ocean * after_y(e, x, s))
            total = t if s == 0 else total
        a_start(p, observe(jnp.concatenate(fields, axis=0)))
        return total

    for buf in (xs1, xs2):
        buf[...] = jnp.zeros(buf.shape, F32)
    block = lax.broadcasted_iota(jnp.int32, (1, LANE), 1) // slots
    place = lax.rem(lax.broadcasted_iota(jnp.int32, (1, LANE), 1), slots)
    for c in range(nch):
        held = jnp.zeros((1, LANE), jnp.int32)
        for i in range(per):
            held = jnp.where(block == i, count[:, per * c + i : per * c + i + 1], held)
        occ[c] = jnp.where(place < held, 1.0, 0.0)
    for n in range(wobs.shape[1]):
        for k, piece in enumerate(split3(wobs[0, n])):
            w3[n, k] = piece
    chunks = weigh([line_up(innov, c) for c in range(nch)])
    pl.semaphore_wait(barrier, nodes - 1)
    a_start(0, chunks)

    ti = lax.broadcasted_iota(jnp.int32, (LANE, LANE), 0)
    tj = lax.broadcasted_iota(jnp.int32, (LANE, LANE), 1)
    for k in range(3):
        tri[0, k * LANE : (k + 1) * LANE] = jnp.where(ti <= tj, 1.0, 0.0).astype(BF16)
        tri[1, k * LANE : (k + 1) * LANE] = jnp.where(ti > tj, 1.0, 0.0).astype(BF16)

    def after(a):
        later = sums_y(a, 1)
        return later + a, later

    rate = ry[...]
    c = sums_y(rate, 0)
    p, b = coefficients(cy, shape_of(rate), c, c[:, :, LANE - 1 :], after)
    for s in every:
        y_send(NXP, s, pick(of_lines(p, s), LANE - 1, s, 0) + pick(of_lines(b, s), 0, s, HALF))
    onehots()
    forth_y(0, zero_row)
    rate = rx[...]
    c = sums_x(rate, False)
    p, b = coefficients(cx, shape_of(rate), c, c[:, SUB - 1 :, :], sums_x_after)
    for s in every:
        put_rows(ob, of_lines(p, s), s)
        put_rows(qb, of_lines(b, s), s)
        x_send(NXP, s, zero_row if s == 0 else None)
    for s in every:
        y_wait(NS * NXP + s)
    for s in every:
        k = NS * NXP + s
        x_wait(xr1, x1_ss, x1_rs, k, s)
        r = x_rows(s)[0]
        whole = xr1[k, 0, 0:r]
        for j in range(1, nx):
            whole = whole * xr1[k, j, 0:r]
        xinv[s, 0:r] = 1.0 / (1.0 - whole)

    forth_x(0)
    rr_part = zero_row
    for s in every:
        x_finish(0, s)
        right = ocean * after_x(s)
        part(res, s)[...] = right
        rr_part = rr_part + inner(right, right)
    rr = None
    alpha = None
    for it in range(ITERS):
        rr_old = rr

        def beside(alpha=alpha, it=it):
            if it == 1:
                sol[...] = alpha * drn[...]
            elif it > 1:
                sol[...] = sol[...] + alpha * drn[...]

        rr = back(2 * it + 1, rr_part, beside)
        direction = res[...]
        if it > 0:
            direction = direction + (rr / rr_old) * drn[...]
        drn[...] = direction
        dd = inner(direction, direction)
        y = a_wait(2 * it + 1)
        if it > 0:
            y = y + (rr / rr_old) * yold[...]
        yold[...] = y
        chunks = weigh(y)
        a_start(2 * it + 2, chunks)
        for k in range(nch):
            dd = dd + y[k] * chunks[k]
        forth_y(2 * it + 2, dd)
        total = forth_x(2 * it + 2)
        alpha = rr / total
        rr_part = zero_row
        for s in every:
            x_finish(2 * it + 2, s)
            new = part(res, s)[...] - alpha * (part(drn, s)[...] + ocean * after_x(s))
            part(res, s)[...] = new
            if it < ITERS - 1:
                rr_part = rr_part + inner(new, new)
        if it == ITERS - 1:
            last = alpha * drn[...]
            sol[...] = last if it == 0 else sol[...] + last


def on_device(nx, ny, rate_x, rate_y, land_mask, obs_cell, obs_count, innovation, obs_weight):
    lev, sx, sy = rate_x.shape
    slots = obs_cell.shape[2]
    nodes = nx * ny
    nch = nodes * slots // LANE
    lines = TR * lev
    assert (sx, sy) == (SUB, LANE) and lines % nx == 0 and lines <= LANE and LANE % slots == 0
    bounds = stages(lines)
    NS = len(bounds)
    rows = [(b - a) // nx for a, b in bounds]
    assert all((b - a) % nx == 0 and b - a < HALF for a, b in bounds)
    M = max(x_message(r, s == 0) for s, r in enumerate(rows))
    Q = NS * (2 * ITERS + 2)
    NXP = 2 * ITERS + 1
    field = (lines, SUB, LANE)
    one = (lev, SUB, LANE)
    vm = pltpu.VMEM
    dma = pltpu.SemaphoreType.DMA
    Rp = (max(rows) + 7) // 8 * 8
    nb, rb = obs_weight.shape[1:3]
    solved, left = pl.pallas_call(
        functools.partial(kernel, nx, ny, lev, slots),
        out_shape=(jax.ShapeDtypeStruct(field, F32),) * 2,
        in_specs=[pl.BlockSpec(memory_space=vm)] * 7,
        out_specs=(pl.BlockSpec(memory_space=vm),) * 2,
        scratch_shapes=[
            vm(field, F32), vm(field, F32),
            vm((lines * SUB, LANE), F32), vm((lines * SUB, LANE), F32),
            vm((6,) + one, F32), vm((6,) + one, F32), vm((2, 3 * LANE, LANE), BF16),
            vm((nb, 3, rb, rb), BF16),
            vm((lines, LANE), F32), vm((lines, LANE), F32),
            vm((lines * SUB, nch * LANE), BF16), vm((LANE, nch * LANE), F32),
            vm((nch, 1, LANE), F32), vm((nch, 1, LANE), F32),
            vm((NS, Rp, LANE), F32),
            vm((NXP, nch, 1, LANE), F32), vm((NXP, nodes, 1, LANE), F32),
            vm((Q, nx, M, LANE), F32), vm((Q, nx, M, LANE), F32),
            vm((Q, nx, M, LANE), F32), vm((Q, nx, M, LANE), F32),
            vm((Q, SUB, LANE), F32), vm((Q, ny, SUB, LANE), F32),
            dma((NXP,)), dma((NXP,)), dma((Q,)), dma((Q,)),
            dma((Q,)), dma((Q,)), dma((Q,)), dma((Q,)),
        ],
        compiler_params=pltpu.CompilerParams(
            collective_id=0, has_side_effects=True, vmem_limit_bytes=56 * 1024 * 1024
        ),
    )(rate_x, rate_y, land_mask, obs_cell, obs_count, innovation, obs_weight)
    shape = (TR, lev, SUB, LANE)
    return solved.reshape(shape), left.reshape(shape)


def solution(mesh):
    placed = (
        P(None, "gx", "gy"),
        P(None, "gx", "gy"),
        P("gx", "gy"),
        P(("gx", "gy"), None, None),
        P(("gx", "gy"), None),
        P(("gx", "gy"), None, None),
        P(("gx", "gy"), None, None, None),
    )
    return jax.shard_map(
        functools.partial(on_device, mesh.shape["gx"], mesh.shape["gy"]),
        mesh=mesh,
        in_specs=placed,
        out_specs=(P(None, None, "gx", "gy"), P(None, None, "gx", "gy")),
        check_vma=False,
    )
```

time: 106 us -> 106 us (level)
  no operation moved by 1% of the time
where the time goes in v3:
time: 106 us
  Pallas kernels  103 us (97%)
  local copies, waits for them, and re-layouts  2.49 us (2%)
    pallas_call x1, Pallas kernels, on_device(): pl.pallas_call(functools.partial(kernel, nx, ny, lev, slots), out_shape=(...  103 us
    unnamed x4, local copies, waits for them, and re-layouts  2.49 us

profile of v3, /device:TPU:0, one launch (start us, length us, event | category | flops | bytes accessed | tf_op | source)
XLA Modules:
  0.0 106.1 jit_solution(5992641685487340025)
XLA Ops:
  0.6 102.9 %shard_map.86 = (f32[80,8,128]{2,1,0:T(8,128)}, f32[80,8,128]{2,1,0:T(8,128)}) custom-call(f32[40,8,128]{2,1,0:T(8,128)} %rx.1, f32[40,8,128]{2,1,0:T(8,128)} %ry.1, s32[8,128]{1,0:T(8,128)} %mask_ref.1, s32[1,32,32]{2,1,0:T(8,128)} %cell.1, s32[1,32]{1,0:T(1,128)} %count.1, f32[1,32,32]{2,1,0:T(8,128)} %innov.1, f32[1,4,256,256]{3,2,1,0:T(8,128)} %wobs.1), custom_call_target="tpu_custom_call" | custom-call | tf_op jit(solution)/shard_map/pallas_call | solution.py:516
  103.6 0.0 copy-start
  103.6 1.8 %copy.11 = f32[2,40,8,128]{3,2,1,0:T(8,128)} copy(f32[2,40,8,128]{3,2,1,0:T(8,128)} %bitcast.3) | data formatting | bytes 655360
  105.3 0.0 copy-done
  105.3 0.7 copy.12
Async XLA Ops:
  103.6 1.8 %copy-start = (f32[80,8,128]{2,1,0:T(8,128)S(1)}, f32[80,8,128]{2,1,0:T(8,128)}, u32[]{:S(2)}) copy-start(f32[80,8,128]{2,1,0:T(8,128)} %get-tuple-element.5) | copy-start | bytes 983044

commit v4 on v2

v4 whole, which is shorter than its diff:
```python
import functools

import jax
import jax.numpy as jnp
from jax import lax
from jax.experimental import pallas as pl
from jax.experimental.pallas import tpu as pltpu
from jax.sharding import PartitionSpec as P

TR = 2
ITERS = 2
SUB = 8
LANE = 128
MESH = pl.DeviceIdType.MESH
F32 = jnp.float32
BF16 = jnp.bfloat16


def split3(a):
    hi = a.astype(BF16)
    rest = a - hi.astype(F32)
    mid = rest.astype(BF16)
    lo = (rest - mid.astype(F32)).astype(BF16)
    return hi, mid, lo


def kernel(
    nx, ny, lev, slots,
    rx, ry, mask_ref, cell, count, innov, wobs,
    sol, res,
    drn, v, v2, vy, ob, qb, ob2, qb2, cx, cy, tri, w3,
    states, rows1h, lanes1h, occ, ydir, yres, xinv,
    as_, ar, xs1, xr1, xs2, xr2, xcs, xcr, ys, yr,
    a_ss, a_rs, x1_ss, x1_rs, x2_ss, x2_rs, xc_ss, xc_rs, y_ss, y_rs,
):
    nodes = nx * ny
    per = LANE // slots
    nch = nodes * slots // LANE
    lines = TR * lev
    R = lines // nx
    mx = lax.axis_index("gx")
    my = lax.axis_index("gy")
    me = mx * ny + my
    NXP = 2 * ITERS + 1
    gxs = [lax.rem(mx + j, nx) for j in range(nx)]
    gys = [lax.rem(my + j, ny) for j in range(ny)]
    others = [(i, j) for i in range(nx) for j in range(ny) if i or j]

    barrier = pltpu.get_barrier_semaphore()
    for i, j in others:
        pl.semaphore_signal(barrier, inc=1, device_id=(gxs[i], gys[j]), device_id_type=MESH)

    one = (lev, SUB, LANE)
    four = (TR, lev, SUB, LANE)
    sub_i = lax.broadcasted_iota(jnp.int32, (SUB, LANE), 0)
    lane_i = lax.broadcasted_iota(jnp.int32, (SUB, LANE), 1)
    ocean = mask_ref[...].astype(F32)

    def sums_x(a, back):
        ax = a.ndim - 2
        for s in (1, 2, 4):
            if back:
                a = a + jnp.where(sub_i < SUB - s, pltpu.roll(a, SUB - s, ax), 0.0)
            else:
                a = a + jnp.where(sub_i >= s, pltpu.roll(a, s, ax), 0.0)
        return a

    def sums_x_after(a):
        b = sums_x(a, True)
        return b, jnp.where(sub_i < SUB - 1, pltpu.roll(b, SUB - 1, a.ndim - 2), 0.0)

    def sums_y(a, which):
        flat = a.reshape(a.size // LANE, LANE)
        lhs = jnp.concatenate(split3(flat), axis=1)
        return jnp.dot(lhs, tri[which], preferred_element_type=F32).reshape(a.shape)

    def shape_of(rate):
        decay = jnp.exp(-rate)
        series = 1.0
        for k in (9, 8, 7, 6, 5, 4, 3, 2):
            series = 1.0 - series * rate * (1.0 / k)
        one_minus = rate * series
        return jnp.sqrt(one_minus * (1.0 + decay)) * jnp.sqrt(jnp.sqrt(one_minus))

    def coefficients(co, w, c, end, after):
        p = jnp.exp(-c)
        pinv = jnp.exp(c)
        p2 = p * p
        total, later = after(p2)
        co[0] = w * pinv
        co[1] = p
        co[2] = w * p
        co[3] = p2
        co[4] = w * (p + pinv * later)
        co[5] = w * jnp.exp(c - end)
        return p, total

    def put_rows(ref, a):
        ref[...] = a.reshape(lines * SUB, LANE)

    def solve_x(u):
        s = sums_x(u * cx[0], False)
        total, later = sums_x_after(s * cx[3])
        return cx[2] * s + cx[0] * later, cx[1] * s, total

    def local_x(u, full):
        field, f, b = solve_x(u)
        v[...] = field
        put_rows(ob, f)
        put_rows(qb, b)
        if full:
            field, f, b = solve_x(ocean * ocean * field)
            v2[...] = field
            put_rows(ob2, f)
            put_rows(qb2, b)

    tag = (
        lax.broadcasted_iota(jnp.int32, four, 3)
        - lax.broadcasted_iota(jnp.int32, four, 0) * lev
        - lax.broadcasted_iota(jnp.int32, four, 1)
    )

    def pick(a, col):
        column = jnp.broadcast_to(a[..., col : col + 1], four)
        return jnp.sum(jnp.where(tag == 0, column, 0.0), axis=(0, 1))

    def local_y(u):
        s = sums_y(u * cy[0], 0)
        m = s * cy[3]
        later = sums_y(m, 1)
        vy[...] = cy[2] * s + cy[0] * later
        return pick(cy[1] * s, LANE - 1), pick(later + m, 0)

    def rows(k):
        return states[k].reshape(TR, lev, 1, LANE)

    def after_x():
        return v[...] + cx[4] * rows(0) + cx[5] * rows(1)

    def after_xx():
        return v2[...] + cx[6] * rows(0) + cx[7] * rows(1) + cx[4] * rows(2) + cx[5] * rows(3)

    def after_y(e, x):
        def columns(a):
            parts = [jnp.broadcast_to(a[:, t : t + 1], (SUB, LANE)) for t in range(lines)]
            return jnp.stack(parts).reshape(four)

        return vy[...] + cy[4] * columns(e) + cy[5] * columns(x)

    zero = jnp.zeros((SUB, LANE), F32)
    zero_row = jnp.zeros((1, LANE), F32)

    def wait_all(buf, sem):
        pltpu.make_async_copy(buf, buf, sem).wait()

    def x_start(src, dst, ss, rs, p, m):
        for i in range(1, nx):
            pltpu.make_async_remote_copy(
                src_ref=src.at[p, gxs[i], pl.ds(0, m)], dst_ref=dst.at[p, mx, pl.ds(0, m)],
                send_sem=ss.at[p], recv_sem=rs.at[p],
                device_id=(gxs[i], my), device_id_type=MESH,
            ).start()
        dst[p, mx] = src[p, mx]

    def x_wait(dst, ss, rs, p, m):
        wait_all(dst.at[p, pl.ds(0, nx - 1), pl.ds(0, m)], rs.at[p])
        wait_all(dst.at[p, pl.ds(0, nx - 1), pl.ds(0, m)], ss.at[p])

    def edge(ref, j, last):
        return ref[pl.ds((SUB - 1 if last else 0) + SUB * R * j, R, stride=SUB), :]

    def x_exchange(p, full):
        m = (R * (4 if full else 2) + SUB - 1) // SUB * SUB
        for j in range(nx):
            xs1[p, j, 0:R] = edge(ob, j, True)
            xs1[p, j, R : 2 * R] = edge(qb, j, False)
            if full:
                xs1[p, j, 2 * R : 3 * R] = edge(ob2, j, True)
                xs1[p, j, 3 * R : 4 * R] = edge(qb2, j, False)
        x_start(xs1, xr1, x1_ss, x1_rs, p, m)
        x_wait(xr1, x1_ss, x1_rs, p, m)

        def got(k):
            return [xr1[p, j, k * R : (k + 1) * R] for j in range(nx)]

        def kept(k):
            return [xcr[0, j, k * R : (k + 1) * R] for j in range(nx)]

        A, C = kept(0), kept(1)
        inv = xinv[0:R]

        def chain(F, B):
            e = F[0]
            for j in range(1, nx):
                e = F[j] + A[j] * e
            e = e * inv
            es, gs, out = [], [], [None] * nx
            for j in range(nx):
                es.append(e)
                gs.append(B[j] + C[j] * e)
                e = F[j] + A[j] * e
            x = gs[nx - 1]
            for j in range(nx - 2, -1, -1):
                x = gs[j] + A[j] * x
            x = x * inv
            for j in range(nx - 1, -1, -1):
                out[j] = x
                x = gs[j] + A[j] * x
            return es, out

        found = list(chain(got(0), got(1)))
        if full:
            es, out = found
            F = [f + a * e + b * x for f, a, b, e, x in zip(got(2), kept(2), kept(3), es, out)]
            B = [f + a * e + b * x for f, a, b, e, x in zip(got(3), kept(4), kept(5), es, out)]
            found += chain(F, B)
        for k, values in enumerate(found):
            for j in range(nx):
                xs2[p, j, k * R : (k + 1) * R] = values[j]
        x_start(xs2, xr2, x2_ss, x2_rs, p, m)
        x_wait(xr2, x2_ss, x2_rs, p, m)
        for k in range(len(found)):
            for j in range(nx):
                states[k, R * j : R * (j + 1)] = xr2[p, j, k * R : (k + 1) * R]

    def y_start(p, f, b):
        ys[p, 0:SUB] = f
        ys[p, SUB : 2 * SUB] = b
        for j in range(1, ny):
            pltpu.make_async_remote_copy(
                src_ref=ys.at[p], dst_ref=yr.at[p, my], send_sem=y_ss.at[p], recv_sem=y_rs.at[p],
                device_id=(mx, gys[j]), device_id_type=MESH,
            ).start()
        yr[p, my] = ys[p]

    def y_wait(p):
        wait_all(yr.at[p, pl.ds(0, ny - 1)], y_rs.at[p])
        wait_all(yr.at[p, pl.ds(0, ny - 1)], y_ss.at[p])

    def y_finish(p):
        y_wait(p)
        e, mine_e, gs = zero, zero, []
        for j in range(ny):
            mine_e = jnp.where(my == j, e, mine_e)
            gs.append(yr[p, j, SUB : 2 * SUB] + yr[NXP, j, SUB : 2 * SUB] * e)
            e = yr[p, j, 0:SUB] + yr[NXP, j, 0:SUB] * e
        x, mine_x = zero, zero
        for j in range(ny - 1, -1, -1):
            mine_x = jnp.where(my == j, x, mine_x)
            x = gs[j] + yr[NXP, j, 0:SUB] * x
        return mine_e, mine_x

    def a_start(p, chunks, row):
        for c in range(nch):
            as_[p, c, 0:1] = chunks[c]
            as_[p, c, 1:2] = row
        for i, j in others:
            pltpu.make_async_remote_copy(
                src_ref=as_.at[p, (gxs[i] * ny + gys[j]) // per], dst_ref=ar.at[p, me],
                send_sem=a_ss.at[p], recv_sem=a_rs.at[p],
                device_id=(gxs[i], gys[j]), device_id_type=MESH,
            ).start()
        ar[p, me] = as_[p, me // per]

    def a_wait(p):
        wait_all(ar.at[p, pl.ds(0, nodes - 1)], a_rs.at[p])
        wait_all(ar.at[p, pl.ds(0, nodes - 1)], a_ss.at[p])
        got = ar[p, :, 0:1, :].reshape(nch, per, 1, LANE)
        block = lax.broadcasted_iota(jnp.int32, (nch, 1, LANE), 2) // slots
        mine = lax.rem(me, per)
        total = jnp.zeros((nch, 1, LANE), F32)
        for i in range(per):
            turned = pltpu.roll(got[:, i], lax.rem(i - mine + per, per) * slots, 2)
            total = jnp.where(block == i, turned, total)
        row = jnp.sum(ar[p, :, 1:2, :], axis=0)
        return total, jnp.broadcast_to(jnp.sum(row, axis=1, keepdims=True), (1, LANE))

    def line_up(ref, c):
        return jnp.concatenate([ref[0, per * c + i : per * c + i + 1, :] for i in range(per)], axis=1)

    def weigh(y):
        per_block = wobs.shape[2] // LANE
        chunks = []
        for n in range(wobs.shape[1]):
            row = jnp.concatenate([y[per_block * n + a] * occ[per_block * n + a] for a in range(per_block)], axis=1)
            which = lax.broadcasted_iota(jnp.int32, (2 * SUB, row.shape[1]), 0)
            lhs = jnp.zeros(which.shape, F32)
            for k, part in enumerate(split3(row)):
                lhs = jnp.where(which == k, part.astype(F32), lhs)
            lhs = lhs.astype(BF16)
            z = jnp.dot(lhs, w3[n, 2], preferred_element_type=F32)
            z = z + jnp.dot(lhs, w3[n, 1], preferred_element_type=F32)
            z = z + jnp.dot(lhs, w3[n, 0], preferred_element_type=F32)
            z = jnp.sum(z, axis=0, keepdims=True)
            for a in range(per_block):
                chunks.append(z[0:1, a * LANE : (a + 1) * LANE] * occ[per_block * n + a])
        return chunks

    def onehots():
        ri = lax.broadcasted_iota(jnp.int32, (lines * SUB, LANE), 0)
        li = lax.broadcasted_iota(jnp.int32, (LANE, LANE), 0)
        for c in range(nch):
            here = line_up(cell, c)
            cols = slice(c * LANE, (c + 1) * LANE)
            rows1h[:, cols] = jnp.where(ri == here // LANE, 1.0, 0.0).astype(BF16)
            lanes1h[:, cols] = jnp.where(li == lax.rem(here, LANE), 1.0, 0.0)

    def observe(field):
        t = jnp.transpose(field.reshape(lines * SUB, LANE))
        lhs = jnp.concatenate(split3(t), axis=0)
        chunks = []
        for c in range(0, nch, 2):
            wide = min(2, nch - c)
            cols = slice(c * LANE, (c + wide) * LANE)
            got = jnp.dot(lhs, rows1h[:, cols], preferred_element_type=F32)
            got = (got[0:LANE] + got[LANE : 2 * LANE]) + got[2 * LANE :]
            got = jnp.sum(got * lanes1h[:, cols], axis=0, keepdims=True)
            chunks += [got[:, k * LANE : (k + 1) * LANE] for k in range(wide)]
        return chunks

    def deposit(vals):
        row = jnp.concatenate([vals[c] for c in range(nch)], axis=1)
        spread = lanes1h[...]
        rhs = jnp.concatenate([(spread * part.astype(F32)).astype(BF16) for part in split3(row)], axis=0)
        got = lax.dot_general(rows1h[...], rhs, (((1,), (1,)), ((), ())), preferred_element_type=F32)
        got = (got[:, 0:LANE] + got[:, LANE : 2 * LANE]) + got[:, 2 * LANE :]
        return got.reshape(four)

    def inner(a, b):
        return jnp.sum(jnp.sum(a * b, axis=(0, 1)), axis=0, keepdims=True)

    def forth(p, full, beside=None):
        vals, total = a_wait(p)
        y_start(p, *local_y(ocean * deposit(vals)))
        if beside is not None:
            beside()
        local_x(after_y(*y_finish(p)), full)
        x_exchange(p, full)
        return total

    def back(p, beside):
        y_start(p, *local_y(after_xx()))
        row = beside()
        a_start(p, observe(ocean * after_y(*y_finish(p))), row)

    for buf in (xs1, xs2, xcs):
        buf[...] = jnp.zeros(buf.shape, F32)
    block = lax.broadcasted_iota(jnp.int32, (1, LANE), 1) // slots
    place = lax.rem(lax.broadcasted_iota(jnp.int32, (1, LANE), 1), slots)
    for c in range(nch):
        held = jnp.zeros((1, LANE), jnp.int32)
        for i in range(per):
            held = jnp.where(block == i, count[:, per * c + i : per * c + i + 1], held)
        occ[c] = jnp.where(place < held, 1.0, 0.0)
    for n in range(wobs.shape[1]):
        for k, piece in enumerate(split3(wobs[0, n])):
            w3[n, k] = piece
    chunks = weigh([line_up(innov, c) for c in range(nch)])
    pl.semaphore_wait(barrier, nodes - 1)
    a_start(0, chunks, zero_row)

    ti = lax.broadcasted_iota(jnp.int32, (LANE, LANE), 0)
    tj = lax.broadcasted_iota(jnp.int32, (LANE, LANE), 1)
    for k in range(3):
        tri[0, k * LANE : (k + 1) * LANE] = jnp.where(ti <= tj, 1.0, 0.0).astype(BF16)
        tri[1, k * LANE : (k + 1) * LANE] = jnp.where(ti > tj, 1.0, 0.0).astype(BF16)

    def after(a):
        later = sums_y(a, 1)
        return later + a, later

    rate = ry[...]
    c = sums_y(rate, 0)
    p, b = coefficients(cy, shape_of(rate), c, c[:, :, LANE - 1 :], after)
    p = jnp.broadcast_to(p[None], four)
    b = jnp.broadcast_to(b[None], four)
    y_start(NXP, pick(p, LANE - 1), pick(b, 0))
    onehots()

    def prepare_x():
        rate = rx[...]
        c = sums_x(rate, False)
        p, b = coefficients(cx, shape_of(rate), c, c[:, SUB - 1 :, :], sums_x_after)
        cx[6], f4, b4 = solve_x(ocean * ocean * cx[4])
        cx[7], f5, b5 = solve_x(ocean * ocean * cx[5])
        for k, (a, last) in enumerate(((p, 1), (b, 0), (f4, 1), (f5, 1), (b4, 0), (b5, 0))):
            buf = (ob, qb)[k % 2]
            put_rows(buf, jnp.stack([a] * TR))
            for j in range(nx):
                xcs[0, j, k * R : (k + 1) * R] = edge(buf, j, last)
        x_start(xcs, xcr, xc_ss, xc_rs, 0, xcs.shape[2])
        y_wait(NXP)

    def finish_x():
        x_wait(xcr, xc_ss, xc_rs, 0, xcs.shape[2])
        whole = xcr[0, 0, 0:R]
        for j in range(1, nx):
            whole = whole * xcr[0, j, 0:R]
        xinv[0:R] = 1.0 / (1.0 - whole)

    vals, _ = a_wait(0)
    y_start(0, *local_y(ocean * deposit(vals)))
    prepare_x()
    local_x(after_y(*y_finish(0)), True)
    finish_x()
    x_exchange(0, True)

    def begin():
        right = ocean * after_x()
        res[...] = right
        drn[...] = right
        return inner(right, right)

    back(1, begin)
    y, rr = a_wait(1)
    ydir[...] = y
    yres[...] = y
    dd = inner(drn[...], drn[...])
    for it in range(ITERS):
        last = it == ITERS - 1
        p = 2 * it + 2
        y = ydir[...]
        chunks = weigh(y)
        row = dd
        for k in range(nch):
            row = row + y[k] * chunks[k]
        a_start(p, chunks, row)
        alpha = rr / forth(p, not last)

        def update():
            d = drn[...]
            sol[...] = alpha * d if it == 0 else sol[...] + alpha * d
            new = res[...] - alpha * (d + ocean * after_x())
            res[...] = new
            return inner(new, new) if not last else None

        if last:
            update()
        else:
            back(p + 1, update)
            t, new_rr = a_wait(p + 1)
            beta = new_rr / rr
            rr = new_rr
            y = yres[...] - alpha * (ydir[...] + t)
            yres[...] = y
            ydir[...] = y + beta * ydir[...]
            d = res[...] + beta * drn[...]
            drn[...] = d
            dd = inner(d, d)


def on_device(nx, ny, rate_x, rate_y, land_mask, obs_cell, obs_count, innovation, obs_weight):
    lev, sx, sy = rate_x.shape
    slots = obs_cell.shape[2]
    nodes = nx * ny
    nch = nodes * slots // LANE
    lines = TR * lev
    assert (sx, sy) == (SUB, LANE) and lines % nx == 0 and lines <= LANE and LANE % slots == 0
    R = lines // nx
    M = (4 * R + 7) // 8 * 8
    MC = (6 * R + 7) // 8 * 8
    NXP = 2 * ITERS + 1
    field = (TR, lev, SUB, LANE)
    one = (lev, SUB, LANE)
    vm = pltpu.VMEM
    dma = pltpu.SemaphoreType.DMA
    Rp = (R + 7) // 8 * 8
    nb, rb = obs_weight.shape[1:3]
    return pl.pallas_call(
        functools.partial(kernel, nx, ny, lev, slots),
        out_shape=(jax.ShapeDtypeStruct(field, F32),) * 2,
        in_specs=[pl.BlockSpec(memory_space=vm)] * 7,
        out_specs=(pl.BlockSpec(memory_space=vm),) * 2,
        scratch_shapes=[
            vm(field, F32), vm(field, F32), vm(field, F32), vm(field, F32),
            vm((lines * SUB, LANE), F32), vm((lines * SUB, LANE), F32),
            vm((lines * SUB, LANE), F32), vm((lines * SUB, LANE), F32),
            vm((8,) + one, F32), vm((6,) + one, F32), vm((2, 3 * LANE, LANE), BF16),
            vm((nb, 3, rb, rb), BF16),
            vm((4, lines, LANE), F32),
            vm((lines * SUB, nch * LANE), BF16), vm((LANE, nch * LANE), F32),
            vm((nch, 1, LANE), F32), vm((nch, 1, LANE), F32), vm((nch, 1, LANE), F32),
            vm((Rp, LANE), F32),
            vm((NXP, nch, 2, LANE), F32), vm((NXP, nodes, 2, LANE), F32),
            vm((NXP, nx, M, LANE), F32), vm((NXP, nx, M, LANE), F32),
            vm((NXP, nx, M, LANE), F32), vm((NXP, nx, M, LANE), F32),
            vm((1, nx, MC, LANE), F32), vm((1, nx, MC, LANE), F32),
            vm((NXP + 1, 2 * SUB, LANE), F32), vm((NXP + 1, ny, 2 * SUB, LANE), F32),
            dma((NXP,)), dma((NXP,)), dma((NXP,)), dma((NXP,)), dma((NXP,)), dma((NXP,)),
            dma((1,)), dma((1,)), dma((NXP + 1,)), dma((NXP + 1,)),
        ],
        compiler_params=pltpu.CompilerParams(
            collective_id=0, has_side_effects=True, vmem_limit_bytes=56 * 1024 * 1024
        ),
    )(rate_x, rate_y, land_mask, obs_cell, obs_count, innovation, obs_weight)


def solution(mesh):
    placed = (
        P(None, "gx", "gy"),
        P(None, "gx", "gy"),
        P("gx", "gy"),
        P(("gx", "gy"), None, None),
        P(("gx", "gy"), None),
        P(("gx", "gy"), None, None),
        P(("gx", "gy"), None, None, None),
    )
    return jax.shard_map(
        functools.partial(on_device, mesh.shape["gx"], mesh.shape["gy"]),
        mesh=mesh,
        in_specs=placed,
        out_specs=(P(None, None, "gx", "gy"), P(None, None, "gx", "gy")),
        check_vma=False,
    )
```

time: 106 us -> 92.9 us (0.88)
  Pallas kernels: 103 us -> 89.5 us
    pallas_call x1, Pallas kernels: 103 us -> 89.5 us  [on_device(): pl.pallas_call(functools.partial(kernel, nx, ny, lev, slots), out_shape=(...]
where the time goes in v4:
time: 92.9 us; the launch traced here: 92.7 us
  Pallas kernels  89.5 us (96%)
  local copies, waits for them, and re-layouts  2.49 us (3%)
    pallas_call x1, Pallas kernels, on_device(): pl.pallas_call(functools.partial(kernel, nx, ny, lev, slots), out_shape=(...  89.5 us
    unnamed x4, local copies, waits for them, and re-layouts  2.49 us

profile of v4, /device:TPU:0, one launch (start us, length us, event | category | flops | bytes accessed | tf_op | source)
XLA Modules:
  0.0 92.7 jit_solution(8592635921181850606)
XLA Ops:
  0.6 89.5 %shard_map.86 = (f32[2,40,8,128]{3,2,1,0:T(8,128)}, f32[2,40,8,128]{3,2,1,0:T(8,128)}) custom-call(f32[40,8,128]{2,1,0:T(8,128)} %rx.1, f32[40,8,128]{2,1,0:T(8,128)} %ry.1, s32[8,128]{1,0:T(8,128)} %mask_ref.1, s32[1,32,32]{2,1,0:T(8,128)} %cell.1, s32[1,32]{1,0:T(1,128)} %count.1, f32[1,32,32]{2,1,0:T(8,128)} %innov.1, f32[1,4,256,256]{3,2,1,0:T(8,128)} %wobs.1), custom_call_target="tpu_custom_call" | custom-call | tf_op jit(solution)/shard_map/pallas_call | solution.py:469
  90.2 0.0 copy-start
  90.2 1.8 %copy.11 = f32[2,40,8,128]{3,2,1,0:T(8,128)} copy(f32[2,40,8,128]{3,2,1,0:T(8,128)} %get-tuple-element.4) | data formatting | bytes 655360
  92.0 0.0 copy-done
  92.0 0.7 copy.12
Async XLA Ops:
  90.2 1.8 %copy-start = (f32[2,40,8,128]{3,2,1,0:T(8,128)S(1)}, f32[2,40,8,128]{3,2,1,0:T(8,128)}, u32[]{:S(2)}) copy-start(f32[2,40,8,128]{3,2,1,0:T(8,128)} %get-tuple-element.5) | copy-start | bytes 983044

commit v5 on v4

--- a/solution.py
+++ b/solution.py
@@ -425,14 +425,22 @@
         for k in range(nch):
             row = row + y[k] * chunks[k]
         a_start(p, chunks, row)
+        if it > 0:
+            drn[...] = res[...] + beta * drn[...]
         alpha = rr / forth(p, not last)
+
+        sums = []
 
         def update():
             d = drn[...]
             sol[...] = alpha * d if it == 0 else sol[...] + alpha * d
             new = res[...] - alpha * (d + ocean * after_x())
             res[...] = new
-            return inner(new, new) if not last else None
+            if last:
+                return None
+            own = inner(new, new)
+            sums.extend((own, inner(new, d)))
+            return own
 
         if last:
             update()
@@ -444,9 +452,7 @@
             y = yres[...] - alpha * (ydir[...] + t)
             yres[...] = y
             ydir[...] = y + beta * ydir[...]
-            d = res[...] + beta * drn[...]
-            drn[...] = d
-            dd = inner(d, d)
+            dd = sums[0] + 2.0 * beta * sums[1] + beta * beta * dd
 
 
 def on_device(nx, ny, rate_x, rate_y, land_mask, obs_cell, obs_count, innovation, obs_weight):

time: 92.9 us -> 92.9 us (level)
  no operation moved by 1% of the time
where the time goes in v5:
time: 92.9 us; the launch traced here: 92.7 us
  Pallas kernels  89.5 us (96%)
  local copies, waits for them, and re-layouts  2.49 us (3%)
    pallas_call x1, Pallas kernels, on_device(): pl.pallas_call(functools.partial(kernel, nx, ny, lev, slots), out_shape=(...  89.5 us
    unnamed x4, local copies, waits for them, and re-layouts  2.49 us

profile of v5, /device:TPU:0, one launch (start us, length us, event | category | flops | bytes accessed | tf_op | source)
XLA Modules:
  0.0 92.7 jit_solution(5931702986951748673)
XLA Ops:
  0.6 89.5 %shard_map.86 = (f32[2,40,8,128]{3,2,1,0:T(8,128)}, f32[2,40,8,128]{3,2,1,0:T(8,128)}) custom-call(f32[40,8,128]{2,1,0:T(8,128)} %rx.1, f32[40,8,128]{2,1,0:T(8,128)} %ry.1, s32[8,128]{1,0:T(8,128)} %mask_ref.1, s32[1,32,32]{2,1,0:T(8,128)} %cell.1, s32[1,32]{1,0:T(1,128)} %count.1, f32[1,32,32]{2,1,0:T(8,128)} %innov.1, f32[1,4,256,256]{3,2,1,0:T(8,128)} %wobs.1), custom_call_target="tpu_custom_call" | custom-call | tf_op jit(solution)/shard_map/pallas_call | solution.py:475
  90.2 0.0 copy-start
  90.2 1.8 %copy.11 = f32[2,40,8,128]{3,2,1,0:T(8,128)} copy(f32[2,40,8,128]{3,2,1,0:T(8,128)} %get-tuple-element.4) | data formatting | bytes 655360
  92.0 0.0 copy-done
  92.0 0.7 copy.12
Async XLA Ops:
  90.2 1.8 %copy-start = (f32[2,40,8,128]{3,2,1,0:T(8,128)S(1)}, f32[2,40,8,128]{3,2,1,0:T(8,128)}, u32[]{:S(2)}) copy-start(f32[2,40,8,128]{3,2,1,0:T(8,128)} %get-tuple-element.5) | copy-start | bytes 983044
